TPU v7x, 128 devices: a whole 4x4x4 slice. The times are simulated.
128 devices in a mesh: section: 2 (over z_hi), dp: 4 (over x), tensor: 16 (over z_lo, y, core).
Axes of the slice: x: 4, y: 4, z: 4 (z_hi: 2, z_lo: 2; z = z_hi * 2 + z_lo), core: 2. Of those that a mesh axis runs over, the one named last changes fastest.
Arguments:
- inputs: bfloat16 [2, 512, 8, 1024], P(None, 'tensor', 'dp'), may hold values from -6 to 6
- lengths: int32 [2, 8], P(None, 'dp'), may hold values from 64 to 512, as said below
- cotangent: bfloat16 [2, 512, 8, 1024], P(None, 'tensor', 'dp'), may hold values from -6 to 6
- w_qkv: bfloat16 [2, 1024, 3, 1024], P('section', None, None, 'tensor'), may hold values from -0.1875 to 0.1875
- b_qv: float32 [2, 2, 1024], P('section', None, 'tensor'), may hold values from -3 to 3
- w_out: bfloat16 [2, 1024, 1024], P('section', 'tensor'), may hold values from -3 to 3
- w_up: bfloat16 [2, 1024, 4096], P('section', None, 'tensor'), may hold values from -0.1875 to 0.1875
- b_up: float32 [2, 4096], P('section', 'tensor'), may hold values from -3 to 3
- w_down: bfloat16 [2, 4096, 1024], P('section', 'tensor'), may hold values from -0.09375 to 0.09375
- norm_gains: float32 [2, 2, 1024], P('section'), may hold values from 0.5 to 1.5
- norm_shifts: float32 [2, 2, 1024], P('section'), may hold values from -3 to 3
- out_bias: float32 [2, 2, 1024], P('section'), may hold values from -3 to 3
Outputs:
- layer_out: bfloat16 [2, 2, 512, 8, 1024], P('section', None, 'tensor', 'dp')
- input_grad: float32 [2, 2, 512, 8, 1024], P('section', None, 'tensor', 'dp')
- grad_qkv: float32 [2, 1024, 3, 1024], P('section', None, None, 'tensor')
- grad_qv: float32 [2, 2, 1024], P('section', None, 'tensor')
- grad_out: float32 [2, 1024, 1024], P('section', 'tensor')
- grad_up: float32 [2, 1024, 4096], P('section', None, 'tensor')
- grad_up_bias: float32 [2, 4096], P('section', 'tensor')
- grad_down: float32 [2, 4096, 1024], P('section', 'tensor')
- grad_gains: float32 [2, 2, 1024], P('section')
- grad_shifts: float32 [2, 2, 1024], P('section')
- grad_out_bias: float32 [2, 2, 1024], P('section')
Inputs may be any that keep to these rules, and one draw needn't show every extreme that they name: `lengths`: valid positions of each sequence, counted from its start. For each index of dp one of its sequences, in one micro-batch drawn from the seed, has all 512.
All inputs are finite; a program needn't handle non-finite values.
Results may differ from a plain program's by a relative error of at most 0.04.
Values may be sent and summed in bfloat16 or wider, within the bound.
A program may use at most 128 MiB of HBM per device.

v0:
```python
import jax
import jax.numpy as jnp
from jax import lax
from jax.sharding import PartitionSpec as P

HEAD = 64


EPSILON = 1e-12
MASKED = -1e30


def from_behind(block, axis, distance):
    devices = range(lax.axis_size(axis))
    route = [(i - distance, i) for i in devices if i - distance in devices]
    return lax.ppermute(block, axis, route)


def normalize(token_rows, gain, shift):
    center = jnp.mean(token_rows, axis=-1, keepdims=True)
    centred = token_rows - center
    spread = jnp.mean(centred * centred, axis=-1, keepdims=True)
    return centred * lax.rsqrt(spread + EPSILON) * gain + shift


def gelu_exact(values_in):
    return jax.nn.gelu(values_in, approximate=False)


def key_scores(query_heads, key_heads, seq_lens):
    scaling = query_heads.shape[-1] ** (-0.5)
    logits = (
        jnp.einsum("tshe,ushe->shtu", query_heads, key_heads, preferred_element_type=jnp.float32)
        * scaling
    )
    positions = lax.broadcasted_iota(jnp.int32, (key_heads.shape[1], key_heads.shape[0]), 1)
    is_valid = positions < seq_lens[:, None]
    return jnp.where(is_valid[:, None, None, :], logits, MASKED)


def layer_forward(row_block, seq_lens, weights):
    w_qkv, b_qv, w_out, w_up, b_up, w_down, norm_gains, norm_shifts, out_bias = weights
    whole_rows = lax.all_gather(row_block, "tensor", axis=0, tiled=True)
    token_count, seq_count = (whole_rows.shape[0], whole_rows.shape[1])
    projected = jnp.einsum("tsd,dch->tsch", whole_rows, w_qkv, preferred_element_type=jnp.float32)
    bias_rows = jnp.stack([b_qv[0], jnp.zeros_like(b_qv[0]), b_qv[1]])
    head_split = (
        (projected + bias_rows).astype(jnp.bfloat16).reshape(token_count, seq_count, 3, -1, HEAD)
    )
    query_heads = head_split[:, :, 0]
    key_heads = head_split[:, :, 1]
    value_heads = head_split[:, :, 2]
    logits = key_scores(query_heads, key_heads, seq_lens)
    row_max = jnp.max(logits, axis=-1, keepdims=True)
    exp_terms = jnp.exp(logits - row_max)
    exp_sum = jnp.sum(exp_terms, axis=-1, keepdims=True)
    log_norm = row_max + jnp.log(exp_sum)
    prob_low = (exp_terms / exp_sum).astype(jnp.bfloat16)
    mixed = jnp.einsum("shtu,ushe->tshe", prob_low, value_heads, preferred_element_type=jnp.float32)
    mixed_low = mixed.reshape(token_count, seq_count, -1).astype(jnp.bfloat16)
    block_piece = mixed_low
    attended = lax.psum_scatter(
        jnp.einsum("tsh,hd->tsd", block_piece, w_out, preferred_element_type=jnp.float32).astype(
            jnp.bfloat16
        ),
        "tensor",
        scatter_dimension=0,
        tiled=True,
    ).astype(jnp.float32)
    first_sum = row_block.astype(jnp.float32) + attended + out_bias[0]
    middle_norm = normalize(first_sum, norm_gains[0], norm_shifts[0])
    middle_rows = lax.all_gather(middle_norm.astype(jnp.bfloat16), "tensor", axis=0, tiled=True)
    pre_act = (
        jnp.einsum("tsd,df->tsf", middle_rows, w_up, preferred_element_type=jnp.float32) + b_up
    )
    hidden = gelu_exact(pre_act).astype(jnp.bfloat16)
    block_piece = hidden
    fed_rows = lax.psum_scatter(
        jnp.einsum("tsf,fd->tsd", block_piece, w_down, preferred_element_type=jnp.float32).astype(
            jnp.bfloat16
        ),
        "tensor",
        scatter_dimension=0,
        tiled=True,
    ).astype(jnp.float32)
    second_sum = middle_norm + fed_rows + out_bias[1]
    result = normalize(second_sum, norm_gains[1], norm_shifts[1])
    saved = (
        whole_rows,
        query_heads,
        key_heads,
        value_heads,
        log_norm,
        mixed_low,
        first_sum,
        middle_rows,
        pre_act,
        hidden,
        second_sum,
        seq_lens,
    )
    return (result, saved)


def layer_backward(grad_rows, weights, saved):
    w_qkv, b_qv, w_out, w_up, b_up, w_down, norm_gains, norm_shifts, out_bias = weights
    (
        whole_rows,
        query_heads,
        key_heads,
        value_heads,
        log_norm,
        mixed_low,
        first_sum,
        middle_rows,
        pre_act,
        hidden,
        second_sum,
        seq_lens,
    ) = saved
    token_count, seq_count = (whole_rows.shape[0], whole_rows.shape[1])
    _, second_back = jax.vjp(normalize, second_sum, norm_gains[1], norm_shifts[1])
    grad_second, gain_two, shift_two = second_back(grad_rows)
    grad_fed = lax.all_gather(grad_second.astype(jnp.bfloat16), "tensor", axis=0, tiled=True)
    grad_down = jnp.einsum("tsf,tsd->fd", hidden, grad_fed, preferred_element_type=jnp.float32)
    grad_hidden = jnp.einsum("tsd,fd->tsf", grad_fed, w_down, preferred_element_type=jnp.float32)
    _, gelu_back = jax.vjp(gelu_exact, pre_act)
    grad_pre = gelu_back(grad_hidden)[0].astype(jnp.bfloat16)
    grad_up_bias = jnp.sum(grad_pre, axis=(0, 1), dtype=jnp.float32)
    grad_up = jnp.einsum("tsd,tsf->df", middle_rows, grad_pre, preferred_element_type=jnp.float32)
    block_piece = grad_pre
    grad_middle = grad_second + lax.psum_scatter(
        jnp.einsum("tsf,df->tsd", block_piece, w_up, preferred_element_type=jnp.float32).astype(
            jnp.bfloat16
        ),
        "tensor",
        scatter_dimension=0,
        tiled=True,
    ).astype(jnp.float32)
    _, first_back = jax.vjp(normalize, first_sum, norm_gains[0], norm_shifts[0])
    grad_first, gain_one, shift_one = first_back(grad_middle)
    grad_attn = lax.all_gather(grad_first.astype(jnp.bfloat16), "tensor", axis=0, tiled=True)
    grad_out = jnp.einsum("tsh,tsd->hd", mixed_low, grad_attn, preferred_element_type=jnp.float32)
    grad_mixed = jnp.einsum("tsd,hd->tsh", grad_attn, w_out, preferred_element_type=jnp.float32)
    grad_mixed = grad_mixed.astype(jnp.bfloat16).reshape(token_count, seq_count, -1, HEAD)
    logits = key_scores(query_heads, key_heads, seq_lens)
    prob_full = jnp.exp(logits - log_norm)
    prob_low = prob_full.astype(jnp.bfloat16)
    grad_value = jnp.einsum(
        "shtu,tshe->ushe", prob_low, grad_mixed, preferred_element_type=jnp.float32
    )
    grad_prob = jnp.einsum(
        "tshe,ushe->shtu", grad_mixed, value_heads, preferred_element_type=jnp.float32
    )
    grad_logits = prob_full * (grad_prob - jnp.sum(prob_full * grad_prob, axis=-1, keepdims=True))
    grad_logits = grad_logits.astype(jnp.bfloat16)
    scaling = HEAD ** (-0.5)
    grad_query = (
        jnp.einsum("shtu,ushe->tshe", grad_logits, key_heads, preferred_element_type=jnp.float32)
        * scaling
    )
    grad_key = (
        jnp.einsum("shtu,tshe->ushe", grad_logits, query_heads, preferred_element_type=jnp.float32)
        * scaling
    )
    grad_proj = jnp.stack([grad_query, grad_key, grad_value], axis=2)
    grad_proj = grad_proj.reshape(token_count, seq_count, 3, -1).astype(jnp.bfloat16)
    bias_terms = jnp.sum(grad_proj, axis=(0, 1), dtype=jnp.float32)
    grad_qv = jnp.stack([bias_terms[0], bias_terms[2]])
    grad_qkv = jnp.einsum(
        "tsd,tsch->dch", whole_rows, grad_proj, preferred_element_type=jnp.float32
    )
    block_piece = grad_proj
    grad_input = grad_first + lax.psum_scatter(
        jnp.einsum("tsch,dch->tsd", block_piece, w_qkv, preferred_element_type=jnp.float32).astype(
            jnp.bfloat16
        ),
        "tensor",
        scatter_dimension=0,
        tiled=True,
    ).astype(jnp.float32)
    out_one = jnp.sum(grad_first, axis=(0, 1))
    out_two = jnp.sum(grad_second, axis=(0, 1))
    weight_terms = (grad_qkv, grad_qv, grad_out, grad_up, grad_up_bias, grad_down)
    norm_terms = (
        jnp.stack([gain_one, gain_two]),
        jnp.stack([shift_one, shift_two]),
        jnp.stack([out_one, out_two]),
    )
    return (grad_input, weight_terms, norm_terms)


def per_device(
    inputs,
    lengths,
    cotangent,
    w_qkv,
    b_qv,
    w_out,
    w_up,
    b_up,
    w_down,
    norm_gains,
    norm_shifts,
    out_bias,
):
    section_count = lax.axis_size("section")
    section_index = lax.axis_index("section")
    weights = tuple(
        (
            param[0]
            for param in (w_qkv, b_qv, w_out, w_up, b_up, w_down, norm_gains, norm_shifts, out_bias)
        )
    )
    micro_count = inputs.shape[0]
    step_count = micro_count + section_count - 1
    received = jnp.zeros(inputs.shape[1:], jnp.bfloat16)
    outputs = []
    saved_steps = []
    for moment in range(step_count):
        own_rows = inputs[min(moment, micro_count - 1)]
        row_block = jnp.where(section_index == 0, own_rows, received)
        micro_index = jnp.clip(moment - section_index, 0, micro_count - 1)
        seq_lens = lax.dynamic_index_in_dim(lengths, micro_index, 0, keepdims=False)
        result, saved = layer_forward(row_block, seq_lens, weights)
        low_out = result.astype(jnp.bfloat16)
        outputs.append(low_out)
        saved_steps.append(saved)
        if moment + 1 < step_count:
            received = from_behind(low_out, "section", 1)
    received = jnp.zeros(inputs.shape[1:], jnp.bfloat16)
    weight_total = None
    norm_total = None
    grads_in = []
    for moment in range(step_count):
        top_index = micro_count - 1 - moment
        if top_index >= 0:
            top_grad = cotangent[top_index]
        else:
            top_grad = jnp.zeros(inputs.shape[1:], jnp.bfloat16)
        grad_rows = jnp.where(section_index == section_count - 1, top_grad, received).astype(
            jnp.float32
        )
        grad_input, weight_terms, norm_terms = layer_backward(
            grad_rows, weights, saved_steps[step_count - 1 - moment]
        )
        grads_in.append(grad_input)
        if moment + 1 < step_count:
            received = from_behind(grad_input.astype(jnp.bfloat16), "section", -1)
        if weight_total is None:
            weight_total = tuple(weight_terms)
            norm_total = tuple(norm_terms)
        else:
            weight_total = jax.tree.map(jnp.add, weight_total, tuple(weight_terms))
            norm_total = jax.tree.map(jnp.add, norm_total, tuple(norm_terms))
    weight_total = (
        lax.psum(weight_total[0].astype(jnp.bfloat16), "dp").astype(jnp.float32),
        lax.psum(weight_total[1].astype(jnp.bfloat16), "dp").astype(jnp.float32),
        lax.psum(weight_total[2].astype(jnp.bfloat16), "dp").astype(jnp.float32),
        lax.psum(weight_total[3].astype(jnp.bfloat16), "dp").astype(jnp.float32),
        lax.psum(weight_total[4].astype(jnp.bfloat16), "dp").astype(jnp.float32),
        lax.psum(weight_total[5].astype(jnp.bfloat16), "dp").astype(jnp.float32),
    )
    norm_total = lax.psum((norm_total[0], norm_total[1], norm_total[2]), ("dp", "tensor"))
    stacked_out = jnp.stack(outputs)
    layer_out = lax.dynamic_slice_in_dim(stacked_out, section_index, micro_count, 0)[None]
    stacked_grads = jnp.stack(grads_in[::-1])
    input_grad = lax.dynamic_slice_in_dim(stacked_grads, section_index, micro_count, 0)[None]
    return (
        layer_out,
        input_grad,
        weight_total[0][None],
        weight_total[1][None],
        weight_total[2][None],
        weight_total[3][None],
        weight_total[4][None],
        weight_total[5][None],
        norm_total[0][None],
        norm_total[1][None],
        norm_total[2][None],
    )


def solution(mesh):
    in_specs = (
        P(None, "tensor", "dp", None),
        P(None, "dp"),
        P(None, "tensor", "dp", None),
        P("section", None, None, "tensor"),
        P("section", None, "tensor"),
        P("section", "tensor", None),
        P("section", None, "tensor"),
        P("section", "tensor"),
        P("section", "tensor", None),
        P("section", None, None),
        P("section", None, None),
        P("section", None, None),
    )
    out_specs = (
        P("section", None, "tensor", "dp", None),
        P("section", None, "tensor", "dp", None),
        P("section", None, None, "tensor"),
        P("section", None, "tensor"),
        P("section", "tensor", None),
        P("section", None, "tensor"),
        P("section", "tensor"),
        P("section", "tensor", None),
        P("section", None, None),
        P("section", None, None),
        P("section", None, None),
    )
    return jax.shard_map(
        per_device, mesh=mesh, in_specs=in_specs, out_specs=out_specs, check_vma=False
    )
```

profile of v0, /device:TPU:1, one launch (start us, length us, event | category | flops | bytes accessed | tf_op | source)
XLA Modules:
  0.0 1588.0 jit_solution(579176796010024216)
XLA Ops:
  11.5 36.3 %all-gather.36.cloned.1.call-done = bf16[1,512,2,1024]{3,1,2,0:T(8,128)(2,1)} async-done(((bf16[1,32,2,1024]{3,1,2,0:T(8,128)(2,1)}), bf16[1,512,2,1024]{3,1,2,0:T(8,128)(2,1)}) %all-gather.36.cloned.1.call-update) | async-done | bytes 2097168 | tf_op jit(solution)/shard_map/all_gather | solution.py:43
  54.6 59.5 %reduce-scatter.13.cloned.1.call-done = bf16[32,2,1024]{2,0,1:T(8,128)(2,1)} async-done(((bf16[512,2,1024]{2,0,1:T(8,128)(2,1)}), bf16[32,2,1024]{2,0,1:T(8,128)(2,1)}) %reduce-scatter.13.cloned.1.call-update) | async-done | bytes 131088 | tf_op jit(solution)/shard_map/reduce_scatter | solution.py:62
  117.9 36.5 %all-gather.14.cloned.1.call-done = bf16[512,2,1024]{2,0,1:T(8,128)(2,1)} async-done(((bf16[32,2,1024]{2,0,1:T(8,128)(2,1)}), bf16[512,2,1024]{2,0,1:T(8,128)(2,1)}) %all-gather.14.cloned.1.call-update) | async-done | bytes 2097168 | tf_op jit(solution)/shard_map/all_gather | solution.py:72
  163.2 59.5 %reduce-scatter.15.cloned.1.call-done = bf16[32,2,1024]{2,0,1:T(8,128)(2,1)} async-done(((bf16[512,2,1024]{2,0,1:T(8,128)(2,1)}), bf16[32,2,1024]{2,0,1:T(8,128)(2,1)}) %reduce-scatter.15.cloned.1.call-update) | async-done | bytes 131088 | tf_op jit(solution)/shard_map/reduce_scatter | solution.py:78
  224.8 4.9 collective-permute-start
  233.1 37.5 %all-gather.16.cloned.1.call-done = bf16[512,2,1024]{2,0,1:T(8,128)(2,1)} async-done(((bf16[32,2,1024]{2,0,1:T(8,128)(2,1)}), bf16[512,2,1024]{2,0,1:T(8,128)(2,1)}) %all-gather.16.cloned.1.call-update) | async-done | bytes 2097168 | tf_op jit(solution)/shard_map/all_gather | solution.py:43
  277.5 59.5 %reduce-scatter.17.cloned.1.call-done = bf16[32,2,1024]{2,0,1:T(8,128)(2,1)} async-done(((bf16[512,2,1024]{2,0,1:T(8,128)(2,1)}), bf16[32,2,1024]{2,0,1:T(8,128)(2,1)}) %reduce-scatter.17.cloned.1.call-update) | async-done | bytes 131088 | tf_op jit(solution)/shard_map/reduce_scatter | solution.py:62
  341.2 36.5 %all-gather.18.cloned.1.call-done = bf16[512,2,1024]{2,0,1:T(8,128)(2,1)} async-done(((bf16[32,2,1024]{2,0,1:T(8,128)(2,1)}), bf16[512,2,1024]{2,0,1:T(8,128)(2,1)}) %all-gather.18.cloned.1.call-update) | async-done | bytes 2097168 | tf_op jit(solution)/shard_map/all_gather | solution.py:72
  386.4 59.5 %reduce-scatter.19.cloned.1.call-done = bf16[32,2,1024]{2,0,1:T(8,128)(2,1)} async-done(((bf16[512,2,1024]{2,0,1:T(8,128)(2,1)}), bf16[32,2,1024]{2,0,1:T(8,128)(2,1)}) %reduce-scatter.19.cloned.1.call-update) | async-done | bytes 131088 | tf_op jit(solution)/shard_map/reduce_scatter | solution.py:78
  449.2 4.9 collective-permute-start.1
  458.4 37.5 %all-gather.20.cloned.1.call-done = bf16[512,2,1024]{2,0,1:T(8,128)(2,1)} async-done(((bf16[32,2,1024]{2,0,1:T(8,128)(2,1)}), bf16[512,2,1024]{2,0,1:T(8,128)(2,1)}) %all-gather.20.cloned.1.call-update) | async-done | bytes 2097168 | tf_op jit(solution)/shard_map/all_gather | solution.py:43
  503.9 59.5 %reduce-scatter.21.cloned.1.call-done = bf16[32,2,1024]{2,0,1:T(8,128)(2,1)} async-done(((bf16[512,2,1024]{2,0,1:T(8,128)(2,1)}), bf16[32,2,1024]{2,0,1:T(8,128)(2,1)}) %reduce-scatter.21.cloned.1.call-update) | async-done | bytes 131088 | tf_op jit(solution)/shard_map/reduce_scatter | solution.py:62
  568.4 36.7 %all-gather.22.cloned.1.call-done = bf16[512,2,1024]{2,0,1:T(8,128)(2,1)} async-done(((bf16[32,2,1024]{2,0,1:T(8,128)(2,1)}), bf16[512,2,1024]{2,0,1:T(8,128)(2,1)}) %all-gather.22.cloned.1.call-update) | async-done | bytes 2097168 | tf_op jit(solution)/shard_map/all_gather | solution.py:72
  616.6 57.7 %reduce-scatter.23.cloned.1.call-done = bf16[32,2,1024]{2,0,1:T(8,128)(2,1)} async-done(((bf16[512,2,1024]{2,0,1:T(8,128)(2,1)}), bf16[32,2,1024]{2,0,1:T(8,128)(2,1)}) %reduce-scatter.23.cloned.1.call-update) | async-done | bytes 131088 | tf_op jit(solution)/shard_map/reduce_scatter | solution.py:78
  680.7 36.7 %all-gather.24.cloned.1.call-done = bf16[512,2,1024]{2,0,1:T(8,128)(2,1)} async-done(((bf16[32,2,1024]{2,0,1:T(8,128)(2,1)}), bf16[512,2,1024]{2,0,1:T(8,128)(2,1)}) %all-gather.24.cloned.1.call-update) | async-done | bytes 2097168 | tf_op jit(solution)/shard_map/all_gather | solution.py:124
  717.4 3.9 convert_reduce_fusion.2
  724.2 59.5 %reduce-scatter.25.cloned.1.call-done = bf16[32,2,1024]{2,0,1:T(8,128)(2,1)} async-done(((bf16[512,2,1024]{2,0,1:T(8,128)(2,1)}), bf16[32,2,1024]{2,0,1:T(8,128)(2,1)}) %reduce-scatter.25.cloned.1.call-update) | async-done | bytes 131088 | tf_op jit(solution)/shard_map/reduce_scatter | solution.py:132
  790.7 35.8 %all-gather.26.cloned.1.call-done = bf16[512,2,1024]{2,0,1:T(8,128)(2,1)} async-done(((bf16[32,2,1024]{2,0,1:T(8,128)(2,1)}), bf16[512,2,1024]{2,0,1:T(8,128)(2,1)}) %all-gather.26.cloned.1.call-update) | async-done | bytes 2097168 | tf_op jit(solution)/shard_map/all_gather | solution.py:142
  834.2 59.4 %reduce-scatter.27.cloned.1.call-done = bf16[32,2,1024]{2,0,1:T(8,128)(2,1)} async-done(((bf16[512,2,1024]{2,0,1:T(8,128)(2,1)}), bf16[32,2,1024]{2,0,1:T(8,128)(2,1)}) %reduce-scatter.27.cloned.1.call-update) | async-done | bytes 131088 | tf_op jit(solution)/shard_map/reduce_scatter | solution.py:174
  896.7 5.9 collective-permute-done.2
  907.1 36.0 %all-gather.28.cloned.1.call-done = bf16[512,2,1024]{2,0,1:T(8,128)(2,1)} async-done(((bf16[32,2,1024]{2,0,1:T(8,128)(2,1)}), bf16[512,2,1024]{2,0,1:T(8,128)(2,1)}) %all-gather.28.cloned.1.call-update) | async-done | bytes 2097168 | tf_op jit(solution)/shard_map/all_gather | solution.py:124
  943.0 3.8 convert_reduce_fusion.1
  949.9 59.5 %reduce-scatter.29.cloned.1.call-done = bf16[32,2,1024]{2,0,1:T(8,128)(2,1)} async-done(((bf16[512,2,1024]{2,0,1:T(8,128)(2,1)}), bf16[32,2,1024]{2,0,1:T(8,128)(2,1)}) %reduce-scatter.29.cloned.1.call-update) | async-done | bytes 131088 | tf_op jit(solution)/shard_map/reduce_scatter | solution.py:132
  1016.2 36.0 %all-gather.30.cloned.1.call-done = bf16[512,2,1024]{2,0,1:T(8,128)(2,1)} async-done(((bf16[32,2,1024]{2,0,1:T(8,128)(2,1)}), bf16[512,2,1024]{2,0,1:T(8,128)(2,1)}) %all-gather.30.cloned.1.call-update) | async-done | bytes 2097168 | tf_op jit(solution)/shard_map/all_gather | solution.py:142
  1059.8 59.6 %reduce-scatter.31.cloned.1.call-done = bf16[32,2,1024]{2,0,1:T(8,128)(2,1)} async-done(((bf16[512,2,1024]{2,0,1:T(8,128)(2,1)}), bf16[32,2,1024]{2,0,1:T(8,128)(2,1)}) %reduce-scatter.31.cloned.1.call-update) | async-done | bytes 131088 | tf_op jit(solution)/shard_map/reduce_scatter | solution.py:174
  1122.5 5.9 collective-permute-done.3
  1130.9 35.7 %all-gather.32.cloned.1.call-done = bf16[512,2,1024]{2,0,1:T(8,128)(2,1)} async-done(((bf16[32,2,1024]{2,0,1:T(8,128)(2,1)}), bf16[512,2,1024]{2,0,1:T(8,128)(2,1)}) %all-gather.32.cloned.1.call-update) | async-done | bytes 2097168 | tf_op jit(solution)/shard_map/all_gather | solution.py:124
  1166.7 3.9 convert_reduce_fusion
  1173.6 59.5 %reduce-scatter.33.cloned.1.call-done = bf16[32,2,1024]{2,0,1:T(8,128)(2,1)} async-done(((bf16[512,2,1024]{2,0,1:T(8,128)(2,1)}), bf16[32,2,1024]{2,0,1:T(8,128)(2,1)}) %reduce-scatter.33.cloned.1.call-update) | async-done | bytes 131088 | tf_op jit(solution)/shard_map/reduce_scatter | solution.py:132
  1257.2 18.5 %all-gather.34.cloned.1.call-done = bf16[512,2,1024]{2,0,1:T(8,128)(2,1)} async-done(((bf16[32,2,1024]{2,0,1:T(8,128)(2,1)}), bf16[512,2,1024]{2,0,1:T(8,128)(2,1)}) %all-gather.34.cloned.1.call-update) | async-done | bytes 2097168 | tf_op jit(solution)/shard_map/all_gather | solution.py:142
  1290.9 273.4 %all-reduce = (f32[1,2,1024]{2,1,0:T(2,128)}, f32[1,2,1024]{2,1,0:T(2,128)}, f32[1,2,1024]{2,1,0:T(2,128)}) all-reduce(f32[1,2,1024]{2,1,0:T(2,128)S(1)} %get-tuple-element.137, f32[1,2,1024]{2,1,0:T(2,128)S(1)} %get-tuple-element.138, f32[1,2,1024]{2,1,0:T(2,128)S(1)} %fusion.200), channel_id=1, replica_groups=mesh['section'=2,'dp'=4,'tensor'=16] {'dp','tensor'}, use_global_device_ids=true, to_apply=%region_63.64 | all-reduce | flops 6144 | bytes 49152 | tf_op jit(solution)/shard_map/psum | solution.py:264
  1564.5 6.1 all-reduce.1
  (525 shorter events, 186.4 us)
Async XLA Ops:
  7.2 40.6 %all-gather.36.cloned.1.call-start = ((), (), s32[]{:S(2)}) async-start(), calls=%async_computation.35 | async-start | bytes 2228224 | tf_op jit(solution)/shard_map/all_gather | solution.py:43
  8.4 223.2 %copy-start.34 = (bf16[1,32,2,1024]{3,2,1,0:T(2,128)(2,1)}, bf16[1,32,2,1024]{3,2,1,0:T(2,128)(2,1)S(1)}, u32[]{:S(2)}) copy-start(bf16[1,32,2,1024]{3,2,1,0:T(2,128)(2,1)S(1)} %get-tuple-element.95) | copy-start | bytes 393220
  9.2 104.9 %reduce-scatter.13.cloned.1.call-start = ((), (), s32[]{:S(2)}) async-start(), calls=%async_computation.12 | async-start | bytes 2228224 | tf_op jit(solution)/shard_map/reduce_scatter | solution.py:62
  54.4 100.1 %all-gather.14.cloned.1.call-start = ((), (), s32[]{:S(2)}) async-start(), calls=%async_computation.13 | async-start | bytes 2228224 | tf_op jit(solution)/shard_map/all_gather | solution.py:72
  54.5 169.6 %copy-start.79 = (f32[1,1,1024]{2,1,0:T(1,128)}, f32[1,1,1024]{2,1,0:T(1,128)S(1)}, u32[]{:S(2)}) copy-start(f32[1,1,1024]{2,1,0:T(1,128)S(1)} %get-tuple-element.99) | copy-start | bytes 12292
  54.6 168.2 %copy-start.81 = (f32[1,1,1024]{2,1,0:T(1,128)}, f32[1,1,1024]{2,1,0:T(1,128)S(1)}, u32[]{:S(2)}) copy-start(f32[1,1,1024]{2,1,0:T(1,128)S(1)} %get-tuple-element.102) | copy-start | bytes 12292
  117.9 104.9 %reduce-scatter.15.cloned.1.call-start = ((), (), s32[]{:S(2)}) async-start(), calls=%async_computation.14 | async-start | bytes 2228224 | tf_op jit(solution)/shard_map/reduce_scatter | solution.py:78
  163.2 107.5 %all-gather.16.cloned.1.call-start = ((), (), s32[]{:S(2)}) async-start(), calls=%async_computation.15 | async-start | bytes 2228224 | tf_op jit(solution)/shard_map/all_gather | solution.py:43
  224.8 6.8 collective-permute-start
  232.3 104.8 %reduce-scatter.17.cloned.1.call-start = ((), (), s32[]{:S(2)}) async-start(), calls=%async_computation.16 | async-start | bytes 2228224 | tf_op jit(solution)/shard_map/reduce_scatter | solution.py:62
  277.5 100.2 %all-gather.18.cloned.1.call-start = ((), (), s32[]{:S(2)}) async-start(), calls=%async_computation.17 | async-start | bytes 2228224 | tf_op jit(solution)/shard_map/all_gather | solution.py:72
  340.9 105.0 %reduce-scatter.19.cloned.1.call-start = ((), (), s32[]{:S(2)}) async-start(), calls=%async_computation.18 | async-start | bytes 2228224 | tf_op jit(solution)/shard_map/reduce_scatter | solution.py:78
  386.3 109.6 %all-gather.20.cloned.1.call-start = ((), (), s32[]{:S(2)}) async-start(), calls=%async_computation.19 | async-start | bytes 2228224 | tf_op jit(solution)/shard_map/all_gather | solution.py:43
  449.2 6.8 collective-permute-start.1
  457.6 105.8 %reduce-scatter.21.cloned.1.call-start = ((), (), s32[]{:S(2)}) async-start(), calls=%async_computation.20 | async-start | bytes 2228224 | tf_op jit(solution)/shard_map/reduce_scatter | solution.py:62
  503.8 101.3 %all-gather.22.cloned.1.call-start = ((), (), s32[]{:S(2)}) async-start(), calls=%async_computation.21 | async-start | bytes 2228224 | tf_op jit(solution)/shard_map/all_gather | solution.py:72
  568.4 105.9 %reduce-scatter.23.cloned.1.call-start = ((), (), s32[]{:S(2)}) async-start(), calls=%async_computation.22 | async-start | bytes 2228224 | tf_op jit(solution)/shard_map/reduce_scatter | solution.py:78
  614.7 102.7 %all-gather.24.cloned.1.call-start = ((), (), s32[]{:S(2)}) async-start(), calls=%async_computation.23 | async-start | bytes 2228224 | tf_op jit(solution)/shard_map/all_gather | solution.py:124
  680.6 103.2 %reduce-scatter.25.cloned.1.call-start = ((), (), s32[]{:S(2)}) async-start(), calls=%async_computation.24 | async-start | bytes 2228224 | tf_op jit(solution)/shard_map/reduce_scatter | solution.py:132
  724.2 102.3 %all-gather.26.cloned.1.call-start = ((), (), s32[]{:S(2)}) async-start(), calls=%async_computation.25 | async-start | bytes 2228224 | tf_op jit(solution)/shard_map/all_gather | solution.py:142
  789.7 103.9 %reduce-scatter.27.cloned.1.call-start = ((), (), s32[]{:S(2)}) async-start(), calls=%async_computation.26 | async-start | bytes 2228224 | tf_op jit(solution)/shard_map/reduce_scatter | solution.py:174
  834.1 108.9 %all-gather.28.cloned.1.call-start = ((), (), s32[]{:S(2)}) async-start(), calls=%async_computation.27 | async-start | bytes 2228224 | tf_op jit(solution)/shard_map/all_gather | solution.py:124
  895.4 7.2 collective-permute-start.2
  907.0 102.4 %reduce-scatter.29.cloned.1.call-start = ((), (), s32[]{:S(2)}) async-start(), calls=%async_computation.28 | async-start | bytes 2228224 | tf_op jit(solution)/shard_map/reduce_scatter | solution.py:132
  949.8 102.4 %all-gather.30.cloned.1.call-start = ((), (), s32[]{:S(2)}) async-start(), calls=%async_computation.29 | async-start | bytes 2228224 | tf_op jit(solution)/shard_map/all_gather | solution.py:142
  1015.4 104.0 %reduce-scatter.31.cloned.1.call-start = ((), (), s32[]{:S(2)}) async-start(), calls=%async_computation.30 | async-start | bytes 2228224 | tf_op jit(solution)/shard_map/reduce_scatter | solution.py:174
  1059.8 106.9 %all-gather.32.cloned.1.call-start = ((), (), s32[]{:S(2)}) async-start(), calls=%async_computation.31 | async-start | bytes 2228224 | tf_op jit(solution)/shard_map/all_gather | solution.py:124
  1121.2 7.2 collective-permute-start.3
  1130.9 102.2 %reduce-scatter.33.cloned.1.call-start = ((), (), s32[]{:S(2)}) async-start(), calls=%async_computation.32 | async-start | bytes 2228224 | tf_op jit(solution)/shard_map/reduce_scatter | solution.py:132
  1173.5 102.1 %all-gather.34.cloned.1.call-start = ((), (), s32[]{:S(2)}) async-start(), calls=%async_computation.33 | async-start | bytes 2228224 | tf_op jit(solution)/shard_map/all_gather | solution.py:142
  1239.0 332.8 %all-reduce.5.cloned.1.call-start = ((), (), s32[]{:S(2)}) async-start(), calls=%async_computation.36 | async-start | bytes 3145728 | tf_op jit(solution)/shard_map/psum | solution.py:257
  1285.8 292.9 %reduce-scatter.35.cloned.1.call-start = ((), (), s32[]{:S(2)}) async-start(), calls=%async_computation.34 | async-start | bytes 2228224 | tf_op jit(solution)/shard_map/reduce_scatter | solution.py:174
  (150 other events, 1702.4 us)
Sparse Core Ops, SparseCore 0:
  10.3 37.4 all-gather.35
  54.5 59.4 reduce-scatter.12
  118.0 36.4 all-gather.13
  163.3 59.4 reduce-scatter.14
  232.4 38.1 all-gather.15
  277.6 59.4 reduce-scatter.16
  341.0 36.5 all-gather.17
  386.5 59.4 reduce-scatter.18
  457.7 38.1 all-gather.19
  503.9 59.4 reduce-scatter.20
  568.5 36.5 all-gather.21
  614.8 59.4 reduce-scatter.22
  680.7 36.5 all-gather.23
  724.3 59.4 reduce-scatter.24
  789.8 36.5 all-gather.25
  834.3 59.3 reduce-scatter.26
  907.1 35.8 all-gather.27
  949.9 59.4 reduce-scatter.28
  1015.6 36.5 all-gather.29
  1059.9 59.4 reduce-scatter.30
  1131.0 35.6 all-gather.31
  1173.6 59.4 reduce-scatter.32
  1239.1 36.5 all-gather.33
  1285.9 50.2 all-reduce.4
  1338.6 59.7 reduce-scatter.34
where the time goes:
time: 1600 us; the launch traced here: 1590 us
  waiting for transfers between devices  1090 us (68%)
  blocking collectives  279 us (17%)
  matrix products  83.9 us (5%)
  other arithmetic  74.1 us (5%)
  local copies, waits for them, and re-layouts  31.6 us (2%)
  between operations  16.1 us (1%)
    psum x1, blocking collectives, per_device(): lax.psum((norm_total[0], norm_total[1], norm_total[2]), ('dp', 'tensor'))  273 us
    reduce_scatter x3, waiting for transfers between devices, layer_backward(): lax.psum_scatter(jnp.einsum('tsf,df->tsd', block_piece, w_up, preferred_e...  179 us
    reduce_scatter x3, waiting for transfers between devices, layer_forward(): lax.psum_scatter(jnp.einsum('tsh,hd->tsd', block_piece, w_out, preferred_...  179 us
    reduce_scatter x3, waiting for transfers between devices, layer_forward(): lax.psum_scatter(jnp.einsum('tsf,fd->tsd', block_piece, w_down, preferred...  177 us
    reduce_scatter x3, waiting for transfers between devices, layer_backward(): lax.psum_scatter(jnp.einsum('tsch,dch->tsd', block_piece, w_qkv, preferre...  119 us
    all_gather x3, waiting for transfers between devices, layer_forward(): whole_rows = lax.all_gather(row_block, 'tensor', axis=0, tiled=True)  111 us
    all_gather x3, waiting for transfers between devices, layer_forward(): lax.all_gather(middle_norm.astype(jnp.bfloat16), 'tensor', axis=0, tiled=...  110 us
    all_gather x3, waiting for transfers between devices, layer_backward(): lax.all_gather(grad_second.astype(jnp.bfloat16), 'tensor', axis=0, tiled=...  108 us
  transfers between devices with their start and end apart: 29, of which 27 were waited for; matrix products, arithmetic and copies ran while one was open for 2% of the time, Pallas kernels for 0%

commit v1 on v0

v1 whole, which is shorter than its diff:
```python
import jax
import jax.numpy as jnp
from jax import lax
from jax.experimental import pallas as pl
from jax.experimental.pallas import tpu as pltpu
from jax.sharding import PartitionSpec as P

EPSILON = 1e-12
MASKED = -1e30
F32 = jnp.float32
BF16 = jnp.bfloat16
MESH = pl.DeviceIdType.MESH
INV_SQRT2 = 0.7071067811865476
INV_SQRT_2PI = 0.3989422804014327
SCALE = 0.125

PIECES_A = ((0, 64), (64, 64), (128, 64), (192, 64))
PIECES_F = ((256, 128), (384, 128), (512, 128), (640, 128))


def nt(a, b):
    return lax.dot_general(a, b, (((1,), (1,)), ((), ())), preferred_element_type=F32)


def nn(a, b):
    return lax.dot_general(a, b, (((1,), (0,)), ((), ())), preferred_element_type=F32)


def standardize(rows):
    center = jnp.mean(rows, axis=-1, keepdims=True)
    centred = rows - center
    spread = jnp.mean(centred * centred, axis=-1, keepdims=True)
    inv = lax.rsqrt(spread + EPSILON)
    return centred * inv, inv


def standardize_back(grad_out, gain, unit, inv):
    scaled = grad_out * gain
    return inv * (
        scaled
        - jnp.mean(scaled, axis=-1, keepdims=True)
        - unit * jnp.mean(scaled * unit, axis=-1, keepdims=True)
    )


def kernel(
    xs, cs, wb, sv, valid,
    lout, igout, gout, smout,
    W, SW, XF, YF, GF, GO, CT, PB, PT, PR, AT, HT, GD, GZT, GPT, GKT, GVT,
    N1, N2, S1, S2, Y1, GR, GY, OWN,
    PART, SIB, SUM, RIN, G, PIN, XIN, FIN, XIF, XIA,
    LO, IG, SM, SMC, SM1, SMY, SM2, SMZ, SM3, SMX,
    ag_s, ag_r, sb_s, sb_r, rs_s, rs_r, in_s, in_r, loc, w_sp, w_sc, w_sf, w_r,
    gp_s, gp_r, gc_s, gc_r, xr_s, xr_r, xg_s, xg_r, lo_s, lo_r, ig_s, ig_r,
    sc_s, sc_r, sy_s, sy_r, sz_s, sz_r, sx_s, sx_r,
):
    zh = lax.axis_index("section")
    x = lax.axis_index("dp")
    t = lax.axis_index("tensor")
    zl = t // 8
    y = (t % 8) // 2
    c = t % 2
    d = t % 8
    z = 2 * zh + zl

    def dev(zh_=None, x_=None, zl_=None, y_=None, c_=None):
        zh_ = zh if zh_ is None else zh_
        x_ = x if x_ is None else x_
        zl_ = zl if zl_ is None else zl_
        y_ = y if y_ is None else y_
        c_ = c if c_ is None else c_
        return (zh_, x_, zl_ * 8 + y_ * 2 + c_)

    def yd(r):
        return dev(y_=lax.rem(y + r, 4))

    def xd(r):
        return dev(x_=lax.rem(x + r, 4))

    sibling = dev(c_=1 - c)
    partner = dev(zl_=1 - zl)
    cross = dev(zh_=1 - zh, zl_=1 - zl)
    far = dev(zh_=1 - zh)

    def rc(src, dst, ssem, rsem, where):
        return pltpu.make_async_remote_copy(
            src_ref=src, dst_ref=dst, send_sem=ssem, recv_sem=rsem, device_id=where, device_id_type=MESH
        )

    def arrived(dst, rsem):
        rc(dst, dst, rsem, rsem, sibling).wait_recv()

    barrier = pltpu.get_barrier_semaphore()
    greeted = [sibling, yd(1), yd(2), yd(3), xd(1), xd(2), xd(3), partner, cross, far]
    for other in greeted:
        pl.semaphore_signal(barrier, inc=1, device_id=other, device_id_type=MESH)
    pl.semaphore_wait(barrier, len(greeted))

    def slot(full, l, yy, cc, half=None):
        if half is None:
            return full.at[l, pl.ds(pl.multiple_of(yy * 128 + cc * 64, 64), 64)]
        return full.at[l, pl.ds(pl.multiple_of(yy * 128 + cc * 64 + half * 32, 32), 32)]

    def ring_ag_start(own, where, s_s, s_r):
        copies = [
            rc(own(0), own(0), s_s(0), s_r(0), where(1)),
            rc(own(1), own(1), s_s(3), s_r(3), where(3)),
            rc(own(1), own(1), s_s(1), s_r(1), where(1)),
            rc(own(0), own(0), s_s(2), s_r(2), where(3)),
        ]
        for cp in copies:
            cp.start()
        return copies

    def ring_ag_finish(slot_of, where, s_s, s_r, landed):
        copies = []
        arrived(slot_of(3, 0), s_r(0))
        cp = rc(slot_of(3, 0), slot_of(3, 0), s_s(4), s_r(4), where(1))
        cp.start()
        copies.append(cp)
        landed(0, 3, 0)
        arrived(slot_of(1, 1), s_r(3))
        cp = rc(slot_of(1, 1), slot_of(1, 1), s_s(5), s_r(5), where(3))
        cp.start()
        copies.append(cp)
        landed(3, 1, 1)
        for k, r, h in ((1, 3, 1), (2, 1, 0), (4, 2, 0), (5, 2, 1)):
            arrived(slot_of(r, h), s_r(k))
            landed(k, r, h)
        return copies

    def gather(full, l, k):
        def at(r, half):
            return slot(full, l, lax.rem(y + r, 4), c, half)

        def s_s(i):
            return ag_s.at[l, k, i]

        def s_r(i):
            return ag_r.at[l, k, i]

        copies = ring_ag_start(lambda half: at(0, half), yd, s_s, s_r)
        mine = slot(full, l, y, c)
        cp = rc(mine, mine, s_s(6), s_r(6), sibling)
        cp.start()
        copies.append(cp)

        def landed(i, r, half):
            got = at(r, half)
            cp = rc(got, got, s_s(7 + i), s_r(7 + i), sibling)
            cp.start()
            copies.append(cp)

        copies += ring_ag_finish(at, yd, s_s, s_r, landed)
        arrived(slot(full, l, y, 1 - c), s_r(6))
        for i, r, half in ((0, 3, 0), (3, 1, 1), (1, 3, 1), (2, 1, 0), (4, 2, 0), (5, 2, 1)):
            arrived(slot(full, l, lax.rem(y + r, 4), 1 - c, half), s_r(7 + i))
        for cp in copies:
            cp.wait_send()

    def rs_two(part, inbox, where, s_s, s_r, h):
        a = rc(part.at[pl.ds(0, h)], inbox.at[0], s_s(0), s_r(0), where(1))
        b = rc(part.at[pl.ds(h, h)], inbox.at[1], s_s(1), s_r(1), where(3))
        a.start()
        b.start()
        return [a, b]

    def rs_forward(one, three, inbox, where, s_s, s_r, h):
        arrived(inbox.at[0], s_r(0))
        one[0:h, :] = (one[0:h, :].astype(F32) + inbox[0].astype(F32)).astype(BF16)
        a = rc(one.at[pl.ds(0, h)], inbox.at[4], s_s(4), s_r(4), where(1))
        a.start()
        arrived(inbox.at[1], s_r(1))
        three[h:, :] = (three[h:, :].astype(F32) + inbox[1].astype(F32)).astype(BF16)
        b = rc(three.at[pl.ds(h, h)], inbox.at[5], s_s(5), s_r(5), where(3))
        b.start()
        return [a, b]

    def rs_last(inbox, s_r):
        for i in (2, 3, 4, 5):
            arrived(inbox.at[i], s_r(i))
        low = inbox[3].astype(F32) + inbox[4].astype(F32)
        high = inbox[2].astype(F32) + inbox[5].astype(F32)
        return jnp.concatenate([low, high], axis=0)

    def scatter(l, k, chunk, window):
        def s_s(i):
            return rs_s.at[l, k, i]

        def s_r(i):
            return rs_r.at[l, k, i]

        copies = []

        def make(r):
            yy = lax.rem(y + r, 4)
            PART[r] = chunk(yy).astype(BF16)
            theirs = PART.at[r, pl.ds(pl.multiple_of((1 - c) * 64, 64), 64)]
            cp = rc(theirs, SIB.at[r], sb_s.at[l, k, r], sb_r.at[l, k, r], sibling)
            cp.start()
            copies.append(cp)

        def both(r):
            arrived(SIB.at[r], sb_r.at[l, k, r])
            mine = PART[r, pl.ds(pl.multiple_of(c * 64, 64), 64), :]
            return mine.astype(F32) + SIB[r].astype(F32)

        make(2)
        make(1)
        SUM[2] = both(2).astype(BF16)
        copies.extend(rs_two(SUM.at[2], RIN, yd, s_s, s_r, 32))
        make(3)
        SUM[1] = both(1).astype(BF16)
        cp = rc(SUM.at[1, pl.ds(32, 32)], RIN.at[2], s_s(2), s_r(2), yd(1))
        cp.start()
        copies.append(cp)
        make(0)
        SUM[3] = both(3).astype(BF16)
        cp = rc(SUM.at[3, pl.ds(0, 32)], RIN.at[3], s_s(3), s_r(3), yd(3))
        cp.start()
        copies.append(cp)
        copies.extend(rs_forward(SUM.at[1], SUM.at[3], RIN, yd, s_s, s_r, 32))
        OWN[...] = both(0)
        window()
        total = OWN[...] + rs_last(RIN, s_r)
        for cp in copies:
            cp.wait_send()
        return total

    def rows_of(ref, base, size):
        return ref.at[pl.ds(base, size)]

    def own_copies(i, where, sems):
        if i == 8:
            return rc(sv, SW.at[z], sems.at[i], w_r.at[zh, zl, i], where)
        base, size = (PIECES_A + PIECES_F)[i]
        return rc(
            rows_of(wb, base, size), W.at[zh, zl, pl.ds(base, size)], sems.at[i], w_r.at[zh, zl, i], where
        )

    order_own = (8, 0, 1, 2, 3, 4, 5, 6, 7)

    def send_own():
        for i in order_own:
            own_copies(i, cross, w_sc).start()
            own_copies(i, partner, w_sp).start()

    def w_at(l, b, i):
        if i == 8:
            return SW.at[2 * l + b]
        base, size = (PIECES_A + PIECES_F)[i]
        return W.at[l, b, pl.ds(base, size)]

    def pass_on(l, pieces):
        @pl.when(zh != l)
        def _():
            for i in pieces:
                got = w_at(l, 1 - zl, i)
                arrived(got, w_r.at[l, 1 - zl, i])
                rc(got, got, w_sf.at[i], w_r.at[l, 1 - zl, i], partner).start()

    def weights_here(l, pieces):
        other = jnp.where(zh == l, 1 - zl, zl)
        for i in pieces:
            arrived(w_at(l, other, i), w_r.at[l, other, i])

    mine_rows = pl.ds(pl.multiple_of(d * 64 + zl * 32, 32), 32)
    x_copy = rc(xs.at[1 - zl], XF.at[0, mine_rows], in_s.at[0], in_r.at[0], partner)
    x_copy.start()
    c_copy = rc(cs.at[1 - zl], CT.at[zl], in_s.at[1], in_r.at[1], partner)

    @pl.when(zh == 0)
    def _():
        send_own()

    c_copy.start()
    w_local = pltpu.make_async_copy(wb, W.at[zh, zl], loc)
    w_local.start()
    SW[z] = sv[...]
    XF[0, mine_rows, :] = xs[zl]
    CT[zl] = cs[zl]
    arrived(XF.at[0, pl.ds(pl.multiple_of(d * 64 + (1 - zl) * 32, 32), 32)], in_r.at[0])
    w_local.wait()

    def spread_out(rows, buf, out, s_s, s_r, l):
        buf[l] = rows.reshape(2, 32, 1024)
        for b in range(2):
            @pl.when((2 * l + b) == z)
            def _(b=b):
                out[z] = buf[l, b]

            @pl.when((2 * l + b) != z)
            def _(b=b):
                rc(buf.at[l, b], out.at[z], s_s.at[l, b], s_r.at[z], dev(zh_=l, zl_=b)).start()

    def spread_wait(buf, out, s_s, s_r):
        for k in range(1, 4):
            zz = lax.rem(z + k, 4)
            arrived(out.at[zz], s_r.at[zz])
        for l in range(2):
            for b in range(2):
                @pl.when((2 * l + b) != z)
                def _(l=l, b=b):
                    rc(buf.at[l, b], buf.at[l, b], s_s.at[l, b], s_r.at[z], sibling).wait_send()

    def row_of(l, i):
        return SW[2 * l, pl.ds(i, 1), :]

    own_rows = pl.ds(pl.multiple_of(d * 64, 64), 64)

    def out_weights(l):
        return jnp.concatenate([W[l, 0, 192:256, :], W[l, 1, 192:256, :]], axis=0)

    def qkv_weights(l):
        return jnp.concatenate([W[l, 0, 0:192, :], W[l, 1, 0:192, :]], axis=0)

    def lanes(yy):
        return pl.ds(pl.multiple_of(yy * 128, 128), 128)

    def forward_layer(l, carry):
        gather(XF, l, 0)

        @pl.when(l == 0)
        def _():
            pass_on(0, (8, 0, 1, 2, 3))

            @pl.when(zh == 1)
            def _():
                send_own()

        weights_here(l, (8, 0, 1, 2, 3))
        qv_bias = SW[2 * l, 7:8, 0:384] + SW[2 * l + 1, 7:8, 0:384]
        proj = (nt(XF[l], qkv_weights(l)) + qv_bias).astype(BF16)
        PB[l] = proj
        PT[l] = proj.T

        def attend(yy):
            cols = lanes(yy)
            for h in range(2):
                base = h * 192
                scores = nn(PB[l, :, base + 64 : base + 128], PT[l, base : base + 64, cols]) * SCALE
                scores = jnp.where(valid[...] > 0.5, scores, MASKED)
                terms = jnp.exp(scores - jnp.max(scores, axis=0, keepdims=True))
                probs = terms * (1.0 / jnp.sum(terms, axis=0, keepdims=True))
                PR[l, h, yy] = probs
                mixed = nn(PT[l, base + 128 : base + 192, :], probs.astype(BF16))
                AT[l, h * 64 : h * 64 + 64, cols] = mixed.astype(BF16)
            return nn(AT[l, :, cols].T, out_weights(l))

        attended = scatter(l, 0, attend, lambda: pass_on(l, (4, 5, 6, 7)))
        unit, inv = standardize(XF[l, own_rows, :].astype(F32) + attended + row_of(l, 4))
        N1[l] = unit
        S1[l] = jnp.broadcast_to(inv, (64, 128))
        middle = unit * row_of(l, 0) + row_of(l, 2)
        Y1[...] = middle
        YF[l, own_rows, :] = middle.astype(BF16)
        gather(YF, l, 1)
        weights_here(l, (4, 5, 6, 7))
        up_bias = SW[2 * l, 6:7, 0:512] + SW[2 * l + 1, 6:7, 0:512]

        def feed(yy):
            rows = YF[l, lanes(yy), :]
            total = None
            for b in range(2):
                pre = nt(rows, W[l, b, 256:512, :]) + up_bias[:, b * 256 : b * 256 + 256]
                cdf = 0.5 * (1.0 + lax.erf(pre * INV_SQRT2))
                hidden = (pre * cdf).astype(BF16)
                GD[l, yy, :, b * 256 : b * 256 + 256] = cdf + pre * (INV_SQRT_2PI * jnp.exp(-0.5 * pre * pre))
                HT[l, b * 256 : b * 256 + 256, lanes(yy)] = hidden.T
                piece = nn(hidden, W[l, b, 512:768, :])
                total = piece if total is None else total + piece
            return total

        def feed_window():
            @pl.when(l == 0)
            def _():
                pass_on(1, (8, 0, 1, 2, 3))

        fed = scatter(l, 1, feed, feed_window)
        unit, inv = standardize(Y1[...] + fed + row_of(l, 5))
        N2[l] = unit
        S2[l] = jnp.broadcast_to(inv, (64, 128))
        result = (unit * row_of(l, 1) + row_of(l, 3)).astype(BF16)

        @pl.when(l == 0)
        def _():
            XF[1, own_rows, :] = result

        spread_out(result, LO, lout, lo_s, lo_r, l)
        return carry

    lax.fori_loop(0, 2, forward_layer, 0)

    arrived(CT.at[1 - zl], in_r.at[1])
    GY[...] = CT[...].reshape(64, 1024).astype(F32)
    SM[...] = jnp.zeros_like(SM)

    A_ROWS, F_ROWS = (0, 256), (256, 512)
    pieces = (A_ROWS, F_ROWS)

    def partner_copy(l, p):
        base, size = pieces[p]
        sel = jnp.where(zh == l, 1 - zl, zl)
        return rc(
            G.at[l, sel, pl.ds(base, size)], PIN.at[l, pl.ds(base, size)], gp_s.at[l, p], gp_r.at[l, p], partner
        )

    def cross_copy(l, p):
        base, size = pieces[p]
        return rc(G.at[l, 1 - zl, pl.ds(base, size)], XIN.at[pl.ds(base, size)], gc_s.at[p], gc_r.at[p], cross)

    def combine(l, p):
        base, size = pieces[p]

        @pl.when(zh != l)
        def _():
            arrived(PIN.at[l, pl.ds(base, size)], gp_r.at[l, p])

            @pl.loop(0, size // 64)
            def _(i):
                rows = pl.ds(pl.multiple_of(base + i * 64, 64), 64)
                G[l, 1 - zl, rows, :] = (G[l, 1 - zl, rows, :].astype(F32) + PIN[l, rows, :].astype(F32)).astype(BF16)

            cross_copy(l, p).start()

    def backward_layer(step, carry):
        l = 1 - step
        grad = GY[...]
        unit = N2[l]
        grad_second = standardize_back(grad, row_of(l, 1), unit, S2[l, :, 0:1])
        SM[l, 1:2, :] = jnp.sum(grad * unit, axis=0, keepdims=True)
        SM[l, 3:4, :] = jnp.sum(grad, axis=0, keepdims=True)
        SM[l, 5:6, :] = jnp.sum(grad_second, axis=0, keepdims=True)
        GR[...] = grad_second
        GF[l, own_rows, :] = grad_second.astype(BF16)
        gather(GF, l, 2)

        def feed_back(yy):
            rows = GF[l, lanes(yy), :]
            total = None
            for b in range(2):
                grad_pre = (nt(rows, W[l, b, 512:768, :]) * GD[l, yy, :, b * 256 : b * 256 + 256]).astype(BF16)
                SM[l, 6:7, b * 256 : b * 256 + 256] += jnp.sum(grad_pre.astype(F32), axis=0, keepdims=True)
                GZT[b * 256 : b * 256 + 256, lanes(yy)] = grad_pre.T
                piece = nn(grad_pre, W[l, b, 256:512, :])
                total = piece if total is None else total + piece
            return total

        def feed_grads():
            @pl.loop(0, 2)
            def _(b):
                rows = pl.ds(pl.multiple_of(b * 256, 256), 256)
                G[l, b, 256:512, :] = nn(GZT[rows, :], YF[l]).astype(BF16)
                G[l, b, 512:768, :] = nn(HT[l, rows, :], GF[l]).astype(BF16)

            partner_copy(l, 1).start()

            @pl.when(l == 0)
            def _():
                combine(1, 0)

        grad_middle = GR[...] + scatter(l, 2, feed_back, feed_grads)
        unit = N1[l]
        grad_first = standardize_back(grad_middle, row_of(l, 0), unit, S1[l, :, 0:1])
        SM[l, 0:1, :] = jnp.sum(grad_middle * unit, axis=0, keepdims=True)
        SM[l, 2:3, :] = jnp.sum(grad_middle, axis=0, keepdims=True)
        SM[l, 4:5, :] = jnp.sum(grad_first, axis=0, keepdims=True)
        GR[...] = grad_first
        GO[l, own_rows, :] = grad_first.astype(BF16)
        gather(GO, l, 3)

        GKT[...] = jnp.zeros_like(GKT)
        GVT[...] = jnp.zeros_like(GVT)

        @pl.loop(0, 4)
        def _(yy):
            cols = lanes(yy)
            grad_mixed = nt(GO[l, cols, :], out_weights(l)).astype(BF16)
            mixed_t = grad_mixed.T
            for h in range(2):
                base = h * 192
                half = mixed_t[h * 64 : h * 64 + 64, :]
                probs = PR[l, h, yy]
                grad_prob = nn(PB[l, :, base + 128 : base + 192], half)
                inner = jnp.sum(probs * grad_prob, axis=0, keepdims=True)
                grad_score = (probs * (grad_prob - inner)).astype(BF16)
                GPT[base : base + 64, cols] = (
                    nn(PT[l, base + 64 : base + 128, :], grad_score) * SCALE
                ).astype(BF16)
                GKT[h] += nt(PT[l, base : base + 64, cols], grad_score)
                GVT[h] += nt(half, probs.astype(BF16))

        for h in range(2):
            base = h * 192
            GPT[base + 64 : base + 128, :] = (GKT[h] * SCALE).astype(BF16)
            GPT[base + 128 : base + 192, :] = GVT[h].astype(BF16)

        def project_back(yy):
            grad_proj = GPT[:, lanes(yy)].T
            SM[l, 7:8, 0:384] += jnp.sum(grad_proj.astype(F32), axis=0, keepdims=True)
            return nn(grad_proj, qkv_weights(l))

        def attend_grads():
            @pl.loop(0, 2)
            def _(b):
                G[l, b, 0:192, :] = nn(GPT[pl.ds(pl.multiple_of(b * 192, 64), 192), :], XF[l]).astype(BF16)
                G[l, b, 192:256, :] = nn(AT[l, pl.ds(pl.multiple_of(b * 64, 64), 64), :], GO[l]).astype(BF16)

            partner_copy(l, 0).start()
            combine(l, 1)

        grad_input = (GR[...] + scatter(l, 3, project_back, attend_grads)).astype(BF16)
        GY[...] = grad_input.astype(F32)
        spread_out(grad_input, IG, igout, ig_s, ig_r, l)
        return carry

    lax.fori_loop(0, 2, backward_layer, 0)

    combine(0, 0)
    row = lax.broadcasted_iota(jnp.int32, (2, 8, 1024), 1)
    cp_c = rc(SM, SMC, sc_s, sc_r, sibling)
    cp_c.start()

    def own_sum(p):
        base, size = pieces[p]
        arrived(PIN.at[zh, pl.ds(base, size)], gp_r.at[zh, p])
        arrived(XIN.at[pl.ds(base, size)], gc_r.at[p])

        @pl.loop(0, size // 64)
        def _(i):
            rows = pl.ds(pl.multiple_of(base + i * 64, 64), 64)
            FIN[rows, :] = (
                G[zh, zl, rows, :].astype(F32) + PIN[zh, rows, :].astype(F32) + XIN[rows, :].astype(F32)
            ).astype(BF16)

    def x_rows(ref, p, r):
        base, size = pieces[p]
        n = size // 4
        return ref.at[pl.ds(pl.multiple_of(base + lax.rem(x + r, 4) * n, n), n)]

    xi = (XIA, XIF)
    done = []

    def x_start(p):
        n = pieces[p][1] // 4
        h = n // 2
        done.extend(rs_two(x_rows(FIN, p, 2), xi[p], xd, lambda i: xr_s.at[p, i], lambda i: xr_r.at[p, i], h))
        a = rc(x_rows(FIN, p, 1).at[pl.ds(h, h)], xi[p].at[2], xr_s.at[p, 2], xr_r.at[p, 2], xd(1))
        b = rc(x_rows(FIN, p, 3).at[pl.ds(0, h)], xi[p].at[3], xr_s.at[p, 3], xr_r.at[p, 3], xd(3))
        a.start()
        b.start()
        done.extend([a, b])

    def x_forward(p):
        h = pieces[p][1] // 8
        done.extend(
            rs_forward(
                x_rows(FIN, p, 1), x_rows(FIN, p, 3), xi[p], xd,
                lambda i: xr_s.at[p, i], lambda i: xr_r.at[p, i], h,
            )
        )

    def x_slot(p):
        base, size = pieces[p]
        n, h = size // 4, size // 8

        def at(r, half):
            start = pl.multiple_of(base + lax.rem(x + r, 4) * n + half * h, h)
            return gout.at[pl.ds(start, h)]

        return at

    def x_last(p):
        base, size = pieces[p]
        n = size // 4
        rows = pl.ds(pl.multiple_of(base + x * n, n), n)
        gout[rows, :] = (FIN[rows, :].astype(F32) + rs_last(xi[p], lambda i: xr_r.at[p, i])).astype(BF16)
        at = x_slot(p)
        done.extend(ring_ag_start(lambda half: at(0, half), xd, lambda i: xg_s.at[p, i], lambda i: xg_r.at[p, i]))

    def x_gather(p):
        done.extend(
            ring_ag_finish(x_slot(p), xd, lambda i: xg_s.at[p, i], lambda i: xg_r.at[p, i], lambda k, r, h: None)
        )

    own_sum(1)
    x_start(1)

    arrived(SMC, sc_r)
    cp_c.wait_send()
    SM1[...] = jnp.where(row < 6, SM[...] + SMC[...], SM[...])
    SMY[y] = SM1[...]
    for r in range(1, 4):
        cp = rc(SM1, SMY.at[y], sy_s.at[r], sy_r.at[r], yd(r))
        cp.start()
        done.append(cp)

    x_forward(1)
    for r in range(1, 4):
        arrived(SMY.at[lax.rem(y + 4 - r, 4)], sy_r.at[r])
    SM2[...] = jnp.where(row < 6, (SMY[0] + SMY[1]) + (SMY[2] + SMY[3]), SM1[...])
    SMZ[z] = SM2[zh]
    for k, where, lz in ((0, partner, zh), (1, cross, 1 - zh), (2, far, 1 - zh)):
        cp = rc(SM2.at[lz], SMZ.at[z], sz_s.at[k], sz_r.at[k], where)
        cp.start()
        done.append(cp)

    own_sum(0)
    x_start(0)
    x_last(1)
    x_forward(0)
    for k, zz in ((0, 2 * zh + 1 - zl), (1, 2 * (1 - zh) + 1 - zl), (2, 2 * (1 - zh) + zl)):
        arrived(SMZ.at[zz], sz_r.at[k])
    SM3[...] = (SMZ[0] + SMZ[1]) + (SMZ[2] + SMZ[3])
    SMX[x] = SM3[...]
    for r in range(1, 4):
        cp = rc(SM3, SMX.at[x], sx_s.at[r], sx_r.at[r], xd(r))
        cp.start()
        done.append(cp)
    x_last(0)
    x_gather(1)
    x_gather(0)
    for r in range(1, 4):
        arrived(SMX.at[lax.rem(x + 4 - r, 4)], sx_r.at[r])
    smout[...] = (SMX[0] + SMX[1]) + (SMX[2] + SMX[3])

    spread_wait(LO, lout, lo_s, lo_r)
    spread_wait(IG, igout, ig_s, ig_r)
    x_copy.wait_send()
    c_copy.wait_send()
    for i in order_own:
        own_copies(i, cross, w_sc).wait_send()
        own_copies(i, partner, w_sp).wait_send()
        got = w_at(1 - zh, 1 - zl, i)
        rc(got, got, w_sf.at[i], w_r.at[1 - zh, 1 - zl, i], partner).wait_send()
    for l in range(2):
        for p in range(2):
            partner_copy(l, p).wait_send()
    for p in range(2):
        cross_copy(1 - zh, p).wait_send()
    for cp in done:
        cp.wait_send()


def run_kernel(xs, cs, wb, sv, valid):
    vm = pltpu.VMEM
    dma = pltpu.SemaphoreType.DMA
    scratch = [
        vm((2, 2, 768, 1024), BF16),
        vm((4, 8, 1024), F32),
        vm((2, 512, 1024), BF16),
        vm((2, 512, 1024), BF16),
        vm((2, 512, 1024), BF16),
        vm((2, 512, 1024), BF16),
        vm((2, 32, 1024), BF16),
        vm((2, 512, 384), BF16),
        vm((2, 384, 512), BF16),
        vm((2, 2, 4, 512, 128), F32),
        vm((2, 128, 512), BF16),
        vm((2, 512, 512), BF16),
        vm((2, 4, 128, 512), F32),
        vm((512, 512), BF16),
        vm((384, 512), BF16),
        vm((2, 64, 512), F32),
        vm((2, 64, 512), F32),
        vm((2, 64, 1024), F32),
        vm((2, 64, 1024), F32),
        vm((2, 64, 128), F32),
        vm((2, 64, 128), F32),
        vm((64, 1024), F32),
        vm((64, 1024), F32),
        vm((64, 1024), F32),
        vm((64, 1024), F32),
        vm((4, 128, 1024), BF16),
        vm((4, 64, 1024), BF16),
        vm((4, 64, 1024), BF16),
        vm((6, 32, 1024), BF16),
        vm((2, 2, 768, 1024), BF16),
        vm((2, 768, 1024), BF16),
        vm((768, 1024), BF16),
        vm((768, 1024), BF16),
        vm((6, 64, 1024), BF16),
        vm((6, 32, 1024), BF16),
        vm((2, 2, 32, 1024), BF16),
        vm((2, 2, 32, 1024), BF16),
        vm((2, 8, 1024), F32),
        vm((2, 8, 1024), F32),
        vm((2, 8, 1024), F32),
        vm((4, 2, 8, 1024), F32),
        vm((2, 8, 1024), F32),
        vm((4, 8, 1024), F32),
        vm((8, 1024), F32),
        vm((4, 8, 1024), F32),
        dma((2, 4, 13)),
        dma((2, 4, 13)),
        dma((2, 4, 4)),
        dma((2, 4, 4)),
        dma((2, 4, 6)),
        dma((2, 4, 6)),
        dma((2,)),
        dma((2,)),
        dma(()),
        dma((9,)),
        dma((9,)),
        dma((9,)),
        dma((2, 2, 9)),
        dma((2, 2)),
        dma((2, 2)),
        dma((2,)),
        dma((2,)),
        dma((2, 6)),
        dma((2, 6)),
        dma((2, 6)),
        dma((2, 6)),
        dma((2, 2)),
        dma((4,)),
        dma((2, 2)),
        dma((4,)),
        dma(()),
        dma(()),
        dma((4,)),
        dma((4,)),
        dma((3,)),
        dma((3,)),
        dma((4,)),
        dma((4,)),
    ]
    in_vmem = pl.BlockSpec(memory_space=pltpu.VMEM)
    return pl.pallas_call(
        kernel,
        out_shape=(
            jax.ShapeDtypeStruct((4, 32, 1024), BF16),
            jax.ShapeDtypeStruct((4, 32, 1024), BF16),
            jax.ShapeDtypeStruct((768, 1024), BF16),
            jax.ShapeDtypeStruct((8, 1024), F32),
        ),
        in_specs=[in_vmem, in_vmem, pl.BlockSpec(memory_space=pl.ANY), in_vmem, in_vmem],
        out_specs=(in_vmem,) * 4,
        scratch_shapes=scratch,
        compiler_params=pltpu.CompilerParams(
            collective_id=0, has_side_effects=True, vmem_limit_bytes=60 * 1024 * 1024
        ),
        cost_estimate=pl.CostEstimate(flops=10_000_000_000, bytes_accessed=10_000_000, transcendentals=3_000_000),
    )(xs, cs, wb, sv, valid)


def per_device(
    inputs, lengths, cotangent, w_qkv, b_qv, w_out, w_up, b_up, w_down, norm_gains, norm_shifts, out_bias
):
    zh = lax.axis_index("section")
    zl = lax.axis_index("tensor") // 8
    xs = jnp.transpose(lax.dynamic_index_in_dim(inputs, zh, 0, keepdims=False), (1, 0, 2))
    cs = jnp.transpose(lax.dynamic_index_in_dim(cotangent, zh, 0, keepdims=False), (1, 0, 2))
    wb = jnp.concatenate(
        [jnp.transpose(w_qkv[0], (1, 2, 0)).reshape(192, 1024), w_out[0], w_up[0].T, w_down[0]], axis=0
    )
    zeros = jnp.zeros((64,), F32)
    up_row = lax.dynamic_update_slice(jnp.zeros((1024,), F32), b_up[0], (zl * 256,))
    qv_row = lax.dynamic_update_slice(
        jnp.zeros((1024,), F32), jnp.concatenate([b_qv[0, 0], zeros, b_qv[0, 1]]), (zl * 192,)
    )
    sv = jnp.concatenate([norm_gains[0], norm_shifts[0], out_bias[0], up_row[None], qv_row[None]], axis=0)
    length = lax.dynamic_slice(lengths, (zh, zl), (1, 1))
    r = lax.broadcasted_iota(jnp.int32, (512, 128), 0)
    position = ((r // 32) % 2) * 256 + (r // 64) * 32 + r % 32
    valid = (position < length).astype(F32)

    lout, igout, g, sm = run_kernel(xs, cs, wb, sv, valid)

    def place(blocks):
        return jnp.transpose(blocks.reshape(2, 2, 32, 1024), (0, 2, 1, 3))[None]

    g32 = g.astype(F32)
    grad_qkv = jnp.transpose(g32[0:192].reshape(3, 64, 1024), (2, 0, 1))[None]
    qv = lax.dynamic_slice(sm[7], (zl * 192,), (192,))
    up_bias = lax.dynamic_slice(sm[6], (zl * 256,), (256,))
    return (
        place(lout),
        place(igout).astype(F32),
        grad_qkv,
        jnp.stack([qv[0:64], qv[128:192]])[None],
        g32[192:256][None],
        g32[256:512].T[None],
        up_bias[None],
        g32[512:768][None],
        sm[0:2][None],
        sm[2:4][None],
        sm[4:6][None],
    )


def solution(mesh):
    in_specs = (
        P(None, "tensor", "dp", None),
        P(None, "dp"),
        P(None, "tensor", "dp", None),
        P("section", None, None, "tensor"),
        P("section", None, "tensor"),
        P("section", "tensor", None),
        P("section", None, "tensor"),
        P("section", "tensor"),
        P("section", "tensor", None),
        P("section", None, None),
        P("section", None, None),
        P("section", None, None),
    )
    out_specs = (
        P("section", None, "tensor", "dp", None),
        P("section", None, "tensor", "dp", None),
        P("section", None, None, "tensor"),
        P("section", None, "tensor"),
        P("section", "tensor", None),
        P("section", None, "tensor"),
        P("section", "tensor"),
        P("section", "tensor", None),
        P("section", None, None),
        P("section", None, None),
        P("section", None, None),
    )
    return jax.shard_map(per_device, mesh=mesh, in_specs=in_specs, out_specs=out_specs, check_vma=False)
```

time: 1600 us -> 322 us (0.20)
  waiting for transfers between devices: 1090 us -> 0 us
  Pallas kernels: 0 us -> 292 us
  blocking collectives: 279 us -> 0 us
  matrix products: 83.9 us -> 0 us
  other arithmetic: 74.1 us -> 6.15 us
    reduce_scatter x12 -> x0, waiting for transfers between devices: 653 us -> none  [the longest x3 179 us: layer_backward(): lax.psum_scatter(jnp.einsum('tsf,df->tsd', block_piece, w_up, preferred_e...]
    all_gather x12 -> x0, waiting for transfers between devices: 420 us -> none  [the longest x3 111 us: layer_forward(): whole_rows = lax.all_gather(row_block, 'tensor', axis=0, tiled=True)]
    pallas_call x0 -> x1, Pallas kernels: none -> 292 us  [run_kernel(): pl.pallas_call(kernel, out_shape=(jax.ShapeDtypeStruct((4, 32, 1024), BF1...]
    psum x2 -> x0, blocking collectives: 279 us -> none  [the longest x1 273 us: per_device(): lax.psum((norm_total[0], norm_total[1], norm_total[2]), ('dp', 'tensor'))]
    dot_general x54 -> x0, matrix products: 83.9 us -> none  [the longest x3 11.6 us: layer_backward(): jnp.einsum('tsd,fd->tsf', grad_fed, w_down, preferred_element_type=jnp.fl...]
    reduce_sum x34 -> x0, other arithmetic: 31.9 us -> none  [the longest x7 9.64 us: normalize(): return centred * lax.rsqrt(spread + EPSILON) * gain + shift]
    unnamed x308 -> x4, local copies, waits for them, and re-layouts: 26.4 us -> 2.56 us
    convert_element_type x15 -> x2, other arithmetic: 19.4 us -> 3 us  [the longest x1 2.62 us: per_device(): valid = (position < length).astype(F32)]
  transfers between devices with their start and end apart: 29 -> 0, of which waited for: 27 -> 0; matrix products, arithmetic and copies ran while one was open for 2% -> 0% of each run, Pallas kernels for 0% -> 0%
where the time goes in v1:
time: 322 us; the launch traced here: 319 us
  Pallas kernels  292 us (91%)
  local copies, waits for them, and re-layouts  20.1 us (6%)
  other arithmetic  6.15 us (2%)
    pallas_call x1, Pallas kernels, run_kernel(): pl.pallas_call(kernel, out_shape=(jax.ShapeDtypeStruct((4, 32, 1024), BF1...  292 us

profile of v1, /device:TPU:1, one launch (start us, length us, event | category | flops | bytes accessed | tf_op | source)
XLA Modules:
  0.0 319.4 jit_solution(3571940733164664809)
XLA Ops:
  0.7 1.3 dynamic_slice.18
  1.9 0.8 slice_bitcast_fusion.7
  2.7 0.1 pad_maximum_fusion.1
  2.8 0.7 constant_dynamic-update-slice_fusion
  3.5 0.1 dynamic_update_slice.9
  3.6 1.4 concatenate.11.sv
  5.0 2.6 fusion.5.valid
  7.6 1.1 constant_dynamic-slice_fusion.3
  8.8 0.7 copy.35
  9.5 0.7 copy.36
  10.1 1.2 copy.25
  11.4 2.5 pad_maximum_fusion.wb
  13.9 292.3 %shard_map.203 = (bf16[4,32,1024]{2,1,0:T(8,128)(2,1)}, bf16[4,32,1024]{2,1,0:T(8,128)(2,1)}, bf16[768,1024]{1,0:T(8,128)(2,1)}, f32[8,1024]{1,0:T(8,128)}) custom-call(bf16[2,32,1024]{2,1,0:T(8,128)(2,1)} %bitcast.73, bf16[2,32,1024]{2,1,0:T(8,128)(2,1)} %bitcast.72, bf16[768,1024]{1,0:T(8,128)(2,1)} %pad_maximum_fusion.wb, f32[8,1024]{1,0:T(8,128)} %concatenate.11.sv, ...), custom_call_target="tpu_custom_call" | custom-call | flops 10000000000 | bytes 10000000 | tf_op jit(solution)/shard_map/pallas_call | solution.py:729
  306.2 0.0 copy-start
  306.2 2.0 copy.34
  308.3 0.8 fusion.14
  309.1 1.5 slice_bitcast_fusion.3
  310.6 0.6 constant_dynamic-slice_fusion.1
  311.2 0.1 constant_dynamic-slice_fusion
  311.2 0.6 maximum_bitcast_fusion
  311.8 2.0 copy.33
  313.8 2.0 slice.54
  315.8 0.0 copy-done
  315.8 0.4 convert_element_type.23
  316.2 0.7 slice_bitcast_fusion.2
  316.9 1.2 slice_bitcast_fusion
  318.1 1.3 copy.28
  (8 shorter events, 0.0 us)
Async XLA Ops:
  306.2 9.6 %copy-start = (bf16[768,1024]{1,0:T(8,128)(2,1)S(1)}, bf16[768,1024]{1,0:T(8,128)(2,1)}, u32[]{:S(2)}) copy-start(bf16[768,1024]{1,0:T(8,128)(2,1)} %get-tuple-element.17) | copy-start | bytes 4718596

commit v2 on v1

v2 whole, which is shorter than its diff:
```python
import jax
import jax.numpy as jnp
from jax import lax
from jax.experimental import pallas as pl
from jax.experimental.pallas import tpu as pltpu
from jax.sharding import PartitionSpec as P

EPSILON = 1e-12
MASKED = -1e30
F32 = jnp.float32
BF16 = jnp.bfloat16
MESH = pl.DeviceIdType.MESH
INV_SQRT2 = 0.7071067811865476
INV_SQRT_2PI = 0.3989422804014327
SCALE = 0.125

PIECES = ((0, 256), (256, 512))


def nt(a, b):
    return lax.dot_general(a, b, (((1,), (1,)), ((), ())), preferred_element_type=F32)


def nn(a, b):
    return lax.dot_general(a, b, (((1,), (0,)), ((), ())), preferred_element_type=F32)


def standardize(rows):
    center = jnp.mean(rows, axis=-1, keepdims=True)
    centred = rows - center
    spread = jnp.mean(centred * centred, axis=-1, keepdims=True)
    inv = lax.rsqrt(spread + EPSILON)
    return centred * inv, inv


def standardize_back(grad_out, gain, unit, inv):
    scaled = grad_out * gain
    return inv * (
        scaled
        - jnp.mean(scaled, axis=-1, keepdims=True)
        - unit * jnp.mean(scaled * unit, axis=-1, keepdims=True)
    )


def kernel(
    xs, cs, wb, sv, valid,
    lout, igout, gout, smout,
    W, SW, XF, YF, GF, GO, CT, PB, PT, PR, AT, HT, GD, GZT, GPT, GKT, GVT,
    N1, N2, S1, S2, Y1, GR, GY, OWN,
    PART, SIB, SUM, RIN, G, GXA, GXF, QXA, QXF, ZXA, ZXF,
    LO, IG, SM, SMC, SM1, SMY, SM2, SMZ, SM3, SMX,
    ag_s, ag_r, sb_s, sb_r, rs_s, rs_r, in_s, in_r, loc, w_s, w_r,
    xr_s, xr_r, gz_s, gz_r, xg_s, xg_r, lo_s, lo_r, ig_s, ig_r,
    sc_s, sc_r, sy_s, sy_r, sz_s, sz_r, sx_s, sx_r,
):
    zh = lax.axis_index("section")
    x = lax.axis_index("dp")
    t = lax.axis_index("tensor")
    zl = t // 8
    y = (t % 8) // 2
    c = t % 2
    d = t % 8
    z = 2 * zh + zl

    def dev(zh_=None, x_=None, zl_=None, y_=None, c_=None):
        zh_ = zh if zh_ is None else zh_
        x_ = x if x_ is None else x_
        zl_ = zl if zl_ is None else zl_
        y_ = y if y_ is None else y_
        c_ = c if c_ is None else c_
        return (zh_, x_, zl_ * 8 + y_ * 2 + c_)

    def yd(r):
        return dev(y_=lax.rem(y + r, 4))

    def xd(r):
        return dev(x_=lax.rem(x + r, 4))

    sibling = dev(c_=1 - c)
    partner = dev(zl_=1 - zl)
    cross = dev(zh_=1 - zh, zl_=1 - zl)
    far = dev(zh_=1 - zh)

    def rc(src, dst, ssem, rsem, where):
        return pltpu.make_async_remote_copy(
            src_ref=src, dst_ref=dst, send_sem=ssem, recv_sem=rsem, device_id=where, device_id_type=MESH
        )

    def arrived(dst, rsem):
        rc(dst, dst, rsem, rsem, sibling).wait_recv()

    barrier = pltpu.get_barrier_semaphore()
    greeted = [sibling, yd(1), yd(2), yd(3), xd(1), xd(2), xd(3), partner, cross, far]
    for other in greeted:
        pl.semaphore_signal(barrier, inc=1, device_id=other, device_id_type=MESH)
    pl.semaphore_wait(barrier, len(greeted))

    def slot(full, l, yy, cc):
        return full.at[l, pl.ds(pl.multiple_of(yy * 128 + cc * 64, 64), 64)]

    def ag_begin(full, l, k):
        mine = slot(full, l, y, c)
        copies = [rc(mine, mine, ag_s.at[l, k, i], ag_r.at[l, k, i], yd(i)) for i in (1, 3, 2)]
        copies.append(rc(mine, mine, ag_s.at[l, k, 4], ag_r.at[l, k, 4], sibling))
        for cp in copies:
            cp.start()
        return copies

    def from_ring(full, l, k, i, copies):
        got = slot(full, l, lax.rem(y + 4 - i, 4), c)
        arrived(got, ag_r.at[l, k, i])
        cp = rc(got, got, ag_s.at[l, k, 4 + i], ag_r.at[l, k, 4 + i], sibling)
        cp.start()
        copies.append(cp)

    def from_sibling(full, l, k, i):
        arrived(slot(full, l, lax.rem(y + 4 - i, 4), 1 - c), ag_r.at[l, k, 4 + i])

    def gather(full, l, k, use):
        copies = ag_begin(full, l, k)
        from_sibling(full, l, k, 0)
        use(y)
        from_ring(full, l, k, 1, copies)
        from_ring(full, l, k, 3, copies)
        from_sibling(full, l, k, 1)
        use(lax.rem(y + 3, 4))
        from_ring(full, l, k, 2, copies)
        from_sibling(full, l, k, 3)
        use(lax.rem(y + 1, 4))
        from_sibling(full, l, k, 2)
        use(lax.rem(y + 2, 4))
        for cp in copies:
            cp.wait_send()

    def make(l, k, r, chunk, copies):
        PART[r] = chunk(lax.rem(y + r, 4)).astype(BF16)
        theirs = PART.at[r, pl.ds(pl.multiple_of((1 - c) * 64, 64), 64)]
        cp = rc(theirs, SIB.at[r], sb_s.at[l, k, r], sb_r.at[l, k, r], sibling)
        cp.start()
        copies.append(cp)

    def both(l, k, r):
        arrived(SIB.at[r], sb_r.at[l, k, r])
        mine = PART[r, pl.ds(pl.multiple_of(c * 64, 64), 64), :]
        return mine.astype(F32) + SIB[r].astype(F32)

    def push(l, k, r, copies):
        SUM[r] = both(l, k, r).astype(BF16)
        cp = rc(SUM.at[r], RIN.at[r], rs_s.at[l, k, r], rs_r.at[l, k, r], yd(r))
        cp.start()
        copies.append(cp)

    def finish(l, k, copies):
        for r in (1, 3, 2):
            arrived(RIN.at[r], rs_r.at[l, k, r])
        total = OWN[...] + ((RIN[1].astype(F32) + RIN[3].astype(F32)) + RIN[2].astype(F32))
        for cp in copies:
            cp.wait_send()
        return total

    def scatter(l, k, chunk, window):
        copies = []
        make(l, k, 2, chunk, copies)
        make(l, k, 1, chunk, copies)
        push(l, k, 2, copies)
        make(l, k, 3, chunk, copies)
        push(l, k, 1, copies)
        make(l, k, 0, chunk, copies)
        push(l, k, 3, copies)
        OWN[...] = both(l, k, 0)
        window()
        return finish(l, k, copies)

    def gather_scatter(full, l, k, chunk, window):
        copies = ag_begin(full, l, k)
        from_sibling(full, l, k, 0)
        make(l, k, 0, chunk, copies)
        from_ring(full, l, k, 1, copies)
        from_ring(full, l, k, 3, copies)
        from_sibling(full, l, k, 1)
        make(l, k, 3, chunk, copies)
        from_ring(full, l, k, 2, copies)
        from_sibling(full, l, k, 3)
        make(l, k, 1, chunk, copies)
        push(l, k, 3, copies)
        from_sibling(full, l, k, 2)
        make(l, k, 2, chunk, copies)
        push(l, k, 1, copies)
        push(l, k, 2, copies)
        OWN[...] = both(l, k, 0)
        window()
        return finish(l, k, copies)

    others = (far, cross, partner)

    def w_at(l, b, i):
        if i == 2:
            return SW.at[2 * l + b]
        base, size = PIECES[i]
        return W.at[l, b, pl.ds(base, size)]

    def w_copy(i, k):
        src = sv if i == 2 else wb.at[pl.ds(*PIECES[i])]
        return rc(src, w_at(zh, zl, i), w_s.at[k, i], w_r.at[zh, zl, i], others[k])

    def send_own(i):
        for k in range(3):
            w_copy(i, k).start()

    def weights_here(l, i):
        for b in range(2):
            @pl.when((2 * l + b) != z)
            def _(b=b):
                arrived(w_at(l, b, i), w_r.at[l, b, i])

    mine_rows = pl.ds(pl.multiple_of(d * 64 + zl * 32, 32), 32)
    x_copy = rc(xs.at[1 - zl], XF.at[0, mine_rows], in_s.at[0], in_r.at[0], partner)
    x_copy.start()
    c_copy = rc(cs.at[1 - zl], CT.at[zl], in_s.at[1], in_r.at[1], partner)

    @pl.when(zh == 0)
    def _():
        send_own(2)
        send_own(0)
        send_own(1)

    c_copy.start()
    w_local = pltpu.make_async_copy(wb, W.at[zh, zl], loc)
    w_local.start()
    SW[z] = sv[...]
    XF[0, mine_rows, :] = xs[zl]
    CT[zl] = cs[zl]
    arrived(XF.at[0, pl.ds(pl.multiple_of(d * 64 + (1 - zl) * 32, 32), 32)], in_r.at[0])
    w_local.wait()

    def spread_out(rows, buf, out, s_s, s_r, l):
        buf[l] = rows.reshape(2, 32, 1024)
        for b in range(2):
            @pl.when((2 * l + b) == z)
            def _(b=b):
                out[z] = buf[l, b]

            @pl.when((2 * l + b) != z)
            def _(b=b):
                rc(buf.at[l, b], out.at[z], s_s.at[l, b], s_r.at[z], dev(zh_=l, zl_=b)).start()

    def spread_wait(buf, out, s_s, s_r):
        for k in range(1, 4):
            zz = lax.rem(z + k, 4)
            arrived(out.at[zz], s_r.at[zz])
        for l in range(2):
            for b in range(2):
                @pl.when((2 * l + b) != z)
                def _(l=l, b=b):
                    rc(buf.at[l, b], buf.at[l, b], s_s.at[l, b], s_r.at[z], sibling).wait_send()

    def row_of(l, i):
        return SW[2 * l, pl.ds(i, 1), :]

    own_rows = pl.ds(pl.multiple_of(d * 64, 64), 64)

    def out_weights(l):
        return jnp.concatenate([W[l, 0, 192:256, :], W[l, 1, 192:256, :]], axis=0)

    def qkv_weights(l):
        return jnp.concatenate([W[l, 0, 0:192, :], W[l, 1, 0:192, :]], axis=0)

    def lanes(yy):
        return pl.ds(pl.multiple_of(yy * 128, 128), 128)

    def forward_layer(l, carry):
        gather(XF, l, 0, lambda yy: None)
        weights_here(l, 2)
        weights_here(l, 0)

        @pl.when((l == 0) & (zh == 1))
        def _():
            send_own(2)
            send_own(0)

        qv_bias = SW[2 * l, 7:8, 0:384] + SW[2 * l + 1, 7:8, 0:384]
        proj = (nt(XF[l], qkv_weights(l)) + qv_bias).astype(BF16)
        PB[l] = proj
        PT[l] = proj.T

        def attend(yy):
            cols = lanes(yy)
            for h in range(2):
                base = h * 192
                scores = nn(PB[l, :, base + 64 : base + 128], PT[l, base : base + 64, cols]) * SCALE
                scores = jnp.where(valid[...] > 0.5, scores, MASKED)
                terms = jnp.exp(scores - jnp.max(scores, axis=0, keepdims=True))
                probs = terms * (1.0 / jnp.sum(terms, axis=0, keepdims=True))
                PR[l, h, yy] = probs
                mixed = nn(PT[l, base + 128 : base + 192, :], probs.astype(BF16))
                AT[l, h * 64 : h * 64 + 64, cols] = mixed.astype(BF16)
            return nn(AT[l, :, cols].T, out_weights(l))

        attended = scatter(l, 0, attend, lambda: None)
        unit, inv = standardize(XF[l, own_rows, :].astype(F32) + attended + row_of(l, 4))
        N1[l] = unit
        S1[l] = jnp.broadcast_to(inv, (64, 128))
        middle = unit * row_of(l, 0) + row_of(l, 2)
        Y1[...] = middle
        YF[l, own_rows, :] = middle.astype(BF16)
        weights_here(l, 1)

        @pl.when((l == 0) & (zh == 1))
        def _():
            send_own(1)

        up_bias = SW[2 * l, 6:7, 0:512] + SW[2 * l + 1, 6:7, 0:512]

        def feed(yy):
            rows = YF[l, lanes(yy), :]
            total = None
            for b in range(2):
                pre = nt(rows, W[l, b, 256:512, :]) + up_bias[:, b * 256 : b * 256 + 256]
                cdf = 0.5 * (1.0 + lax.erf(pre * INV_SQRT2))
                hidden = (pre * cdf).astype(BF16)
                GD[l, yy, :, b * 256 : b * 256 + 256] = cdf + pre * (INV_SQRT_2PI * jnp.exp(-0.5 * pre * pre))
                HT[l, b * 256 : b * 256 + 256, lanes(yy)] = hidden.T
                piece = nn(hidden, W[l, b, 512:768, :])
                total = piece if total is None else total + piece
            return total

        fed = gather_scatter(YF, l, 1, feed, lambda: None)
        unit, inv = standardize(Y1[...] + fed + row_of(l, 5))
        N2[l] = unit
        S2[l] = jnp.broadcast_to(inv, (64, 128))
        result = (unit * row_of(l, 1) + row_of(l, 3)).astype(BF16)

        @pl.when(l == 0)
        def _():
            XF[1, own_rows, :] = result

        spread_out(result, LO, lout, lo_s, lo_r, l)
        return carry

    lax.fori_loop(0, 2, forward_layer, 0)

    arrived(CT.at[1 - zl], in_r.at[1])
    GY[...] = CT[...].reshape(64, 1024).astype(F32)
    SM[...] = jnp.zeros_like(SM)

    GX, QX, ZX = (GXA, GXF), (QXA, QXF), (ZXA, ZXF)

    def own_part(p, ref, who, *lead):
        base, size = PIECES[p]
        n = size // 4
        return ref.at[(*lead, pl.ds(pl.multiple_of(base + who * n, n), n))]

    def x_copy_of(l, p, b, r):
        src = own_part(p, G, lax.rem(x + r, 4), l, b)
        return rc(src, GX[p].at[l, b, r - 1], xr_s.at[l, p, b, r - 1], xr_r.at[l, p, b, r - 1], xd(r))

    def z_copy_of(l, p, b):
        k = lax.rem(2 * l + b + 4 - z, 4) - 1
        return rc(QX[p].at[l, b], ZX[p].at[k], gz_s.at[l, p, b], gz_r.at[p, k], dev(zh_=l, zl_=b))

    def g_copy_of(p, r):
        mine = own_part(p, gout, x)
        return rc(mine, mine, xg_s.at[p, r - 1], xg_r.at[p, r - 1], xd(r))

    def grad_x(l, p):
        for b in range(2):
            for r in (2, 1, 3):
                x_copy_of(l, p, b, r).start()

    def grad_z(l, p):
        n = PIECES[p][1] // 4
        for b in range(2):
            for r in (1, 3, 2):
                arrived(GX[p].at[l, b, r - 1], xr_r.at[l, p, b, r - 1])
            mine = own_part(p, G, x, l, b)

            @pl.loop(0, n // 32)
            def _(i, b=b, mine=mine):
                rows = pl.ds(pl.multiple_of(i * 32, 32), 32)
                QX[p][l, b, rows, :] = (
                    (mine[rows, :].astype(F32) + GX[p][l, b, 0, rows, :].astype(F32))
                    + (GX[p][l, b, 1, rows, :].astype(F32) + GX[p][l, b, 2, rows, :].astype(F32))
                ).astype(BF16)

            @pl.when((2 * l + b) != z)
            def _(b=b):
                z_copy_of(l, p, b).start()

    def grad_own(p):
        n = PIECES[p][1] // 4
        for k in range(3):
            arrived(ZX[p].at[k], gz_r.at[p, k])
        mine = own_part(p, gout, x)

        @pl.loop(0, n // 32)
        def _(i):
            rows = pl.ds(pl.multiple_of(i * 32, 32), 32)
            mine[rows, :] = (
                (QX[p][zh, zl, rows, :].astype(F32) + ZX[p][0, rows, :].astype(F32))
                + (ZX[p][1, rows, :].astype(F32) + ZX[p][2, rows, :].astype(F32))
            ).astype(BF16)

        for r in (2, 1, 3):
            g_copy_of(p, r).start()

    def grad_done(p):
        for r in (1, 3, 2):
            arrived(own_part(p, gout, lax.rem(x + 4 - r, 4)), xg_r.at[p, r - 1])

    def backward_layer(step, carry):
        l = 1 - step
        grad = GY[...]
        unit = N2[l]
        grad_second = standardize_back(grad, row_of(l, 1), unit, S2[l, :, 0:1])
        SM[l, 1:2, :] = jnp.sum(grad * unit, axis=0, keepdims=True)
        SM[l, 3:4, :] = jnp.sum(grad, axis=0, keepdims=True)
        SM[l, 5:6, :] = jnp.sum(grad_second, axis=0, keepdims=True)
        GR[...] = grad_second
        GF[l, own_rows, :] = grad_second.astype(BF16)
        def feed_back(yy):
            rows = GF[l, lanes(yy), :]
            total = None
            for b in range(2):
                grad_pre = (nt(rows, W[l, b, 512:768, :]) * GD[l, yy, :, b * 256 : b * 256 + 256]).astype(BF16)
                SM[l, 6:7, b * 256 : b * 256 + 256] += jnp.sum(grad_pre.astype(F32), axis=0, keepdims=True)
                GZT[b * 256 : b * 256 + 256, lanes(yy)] = grad_pre.T
                piece = nn(grad_pre, W[l, b, 256:512, :])
                total = piece if total is None else total + piece
            return total

        def feed_grads():
            @pl.loop(0, 2)
            def _(b):
                rows = pl.ds(pl.multiple_of(b * 256, 256), 256)
                G[l, b, 256:512, :] = nn(GZT[rows, :], YF[l]).astype(BF16)
                G[l, b, 512:768, :] = nn(HT[l, rows, :], GF[l]).astype(BF16)

            grad_x(l, 1)

            @pl.when(l == 0)
            def _():
                grad_z(1, 1)
                grad_z(1, 0)

        grad_middle = GR[...] + gather_scatter(GF, l, 2, feed_back, feed_grads)
        unit = N1[l]
        grad_first = standardize_back(grad_middle, row_of(l, 0), unit, S1[l, :, 0:1])
        SM[l, 0:1, :] = jnp.sum(grad_middle * unit, axis=0, keepdims=True)
        SM[l, 2:3, :] = jnp.sum(grad_middle, axis=0, keepdims=True)
        SM[l, 4:5, :] = jnp.sum(grad_first, axis=0, keepdims=True)
        GR[...] = grad_first
        GO[l, own_rows, :] = grad_first.astype(BF16)
        GKT[...] = jnp.zeros_like(GKT)
        GVT[...] = jnp.zeros_like(GVT)

        def attend_back(yy):
            cols = lanes(yy)
            grad_mixed = nt(GO[l, cols, :], out_weights(l)).astype(BF16)
            mixed_t = grad_mixed.T
            for h in range(2):
                base = h * 192
                half = mixed_t[h * 64 : h * 64 + 64, :]
                probs = PR[l, h, yy]
                grad_prob = nn(PB[l, :, base + 128 : base + 192], half)
                inner = jnp.sum(probs * grad_prob, axis=0, keepdims=True)
                grad_score = (probs * (grad_prob - inner)).astype(BF16)
                GPT[base : base + 64, cols] = (
                    nn(PT[l, base + 64 : base + 128, :], grad_score) * SCALE
                ).astype(BF16)
                GKT[h] += nt(PT[l, base : base + 64, cols], grad_score)
                GVT[h] += nt(half, probs.astype(BF16))

        gather(GO, l, 3, attend_back)

        for h in range(2):
            base = h * 192
            GPT[base + 64 : base + 128, :] = (GKT[h] * SCALE).astype(BF16)
            GPT[base + 128 : base + 192, :] = GVT[h].astype(BF16)

        def project_back(yy):
            grad_proj = GPT[:, lanes(yy)].T
            SM[l, 7:8, 0:384] += jnp.sum(grad_proj.astype(F32), axis=0, keepdims=True)
            return nn(grad_proj, qkv_weights(l))

        def attend_grads():
            @pl.loop(0, 2)
            def _(b):
                G[l, b, 0:192, :] = nn(GPT[pl.ds(pl.multiple_of(b * 192, 64), 192), :], XF[l]).astype(BF16)
                G[l, b, 192:256, :] = nn(AT[l, pl.ds(pl.multiple_of(b * 64, 64), 64), :], GO[l]).astype(BF16)

            grad_x(l, 0)

        grad_input = (GR[...] + scatter(l, 3, project_back, attend_grads)).astype(BF16)
        GY[...] = grad_input.astype(F32)
        spread_out(grad_input, IG, igout, ig_s, ig_r, l)
        return carry

    lax.fori_loop(0, 2, backward_layer, 0)

    done = []

    def go(cp):
        cp.start()
        done.append(cp)

    row = lax.broadcasted_iota(jnp.int32, (2, 8, 1024), 1)
    go(rc(SM, SMC, sc_s, sc_r, sibling))
    grad_z(0, 1)
    arrived(SMC, sc_r)
    SM1[...] = jnp.where(row < 6, SM[...] + SMC[...], SM[...])
    SMY[y] = SM1[...]
    for r in range(1, 4):
        go(rc(SM1, SMY.at[y], sy_s.at[r], sy_r.at[r], yd(r)))
    grad_z(0, 0)
    for r in range(1, 4):
        arrived(SMY.at[lax.rem(y + 4 - r, 4)], sy_r.at[r])
    SM2[...] = jnp.where(row < 6, (SMY[0] + SMY[1]) + (SMY[2] + SMY[3]), SM1[...])
    SMZ[z] = SM2[zh]
    for k, where, lz in ((0, partner, zh), (1, cross, 1 - zh), (2, far, 1 - zh)):
        go(rc(SM2.at[lz], SMZ.at[z], sz_s.at[k], sz_r.at[k], where))
    grad_own(1)
    for k, zz in ((0, 2 * zh + 1 - zl), (1, 2 * (1 - zh) + 1 - zl), (2, 2 * (1 - zh) + zl)):
        arrived(SMZ.at[zz], sz_r.at[k])
    SM3[...] = (SMZ[0] + SMZ[1]) + (SMZ[2] + SMZ[3])
    SMX[x] = SM3[...]
    for r in range(1, 4):
        go(rc(SM3, SMX.at[x], sx_s.at[r], sx_r.at[r], xd(r)))
    grad_own(0)
    for r in range(1, 4):
        arrived(SMX.at[lax.rem(x + 4 - r, 4)], sx_r.at[r])
    smout[...] = (SMX[0] + SMX[1]) + (SMX[2] + SMX[3])
    spread_wait(LO, lout, lo_s, lo_r)
    spread_wait(IG, igout, ig_s, ig_r)
    grad_done(1)
    grad_done(0)

    x_copy.wait_send()
    c_copy.wait_send()
    for i in range(3):
        for k in range(3):
            w_copy(i, k).wait_send()
    for p in range(2):
        for l in range(2):
            for b in range(2):
                for r in range(1, 4):
                    x_copy_of(l, p, b, r).wait_send()

                @pl.when((2 * l + b) != z)
                def _(l=l, b=b, p=p):
                    z_copy_of(l, p, b).wait_send()
        for r in range(1, 4):
            g_copy_of(p, r).wait_send()
    for cp in done:
        cp.wait_send()


def run_kernel(xs, cs, wb, sv, valid):
    vm = pltpu.VMEM
    dma = pltpu.SemaphoreType.DMA
    scratch = [
        vm((2, 2, 768, 1024), BF16),
        vm((4, 8, 1024), F32),
        vm((2, 512, 1024), BF16),
        vm((2, 512, 1024), BF16),
        vm((2, 512, 1024), BF16),
        vm((2, 512, 1024), BF16),
        vm((2, 32, 1024), BF16),
        vm((2, 512, 384), BF16),
        vm((2, 384, 512), BF16),
        vm((2, 2, 4, 512, 128), F32),
        vm((2, 128, 512), BF16),
        vm((2, 512, 512), BF16),
        vm((2, 4, 128, 512), F32),
        vm((512, 512), BF16),
        vm((384, 512), BF16),
        vm((2, 64, 512), F32),
        vm((2, 64, 512), F32),
        vm((2, 64, 1024), F32),
        vm((2, 64, 1024), F32),
        vm((2, 64, 128), F32),
        vm((2, 64, 128), F32),
        vm((64, 1024), F32),
        vm((64, 1024), F32),
        vm((64, 1024), F32),
        vm((64, 1024), F32),
        vm((4, 128, 1024), BF16),
        vm((4, 64, 1024), BF16),
        vm((4, 64, 1024), BF16),
        vm((4, 64, 1024), BF16),
        vm((2, 2, 768, 1024), BF16),
        vm((2, 2, 3, 64, 1024), BF16),
        vm((2, 2, 3, 128, 1024), BF16),
        vm((2, 2, 64, 1024), BF16),
        vm((2, 2, 128, 1024), BF16),
        vm((3, 64, 1024), BF16),
        vm((3, 128, 1024), BF16),
        vm((2, 2, 32, 1024), BF16),
        vm((2, 2, 32, 1024), BF16),
        vm((2, 8, 1024), F32),
        vm((2, 8, 1024), F32),
        vm((2, 8, 1024), F32),
        vm((4, 2, 8, 1024), F32),
        vm((2, 8, 1024), F32),
        vm((4, 8, 1024), F32),
        vm((8, 1024), F32),
        vm((4, 8, 1024), F32),
        dma((2, 4, 8)),
        dma((2, 4, 8)),
        dma((2, 4, 4)),
        dma((2, 4, 4)),
        dma((2, 4, 4)),
        dma((2, 4, 4)),
        dma((2,)),
        dma((2,)),
        dma(()),
        dma((3, 3)),
        dma((2, 2, 3)),
        dma((2, 2, 2, 3)),
        dma((2, 2, 2, 3)),
        dma((2, 2, 2)),
        dma((2, 3)),
        dma((2, 3)),
        dma((2, 3)),
        dma((2, 2)),
        dma((4,)),
        dma((2, 2)),
        dma((4,)),
        dma(()),
        dma(()),
        dma((4,)),
        dma((4,)),
        dma((3,)),
        dma((3,)),
        dma((4,)),
        dma((4,)),
    ]
    in_vmem = pl.BlockSpec(memory_space=pltpu.VMEM)
    return pl.pallas_call(
        kernel,
        out_shape=(
            jax.ShapeDtypeStruct((4, 32, 1024), BF16),
            jax.ShapeDtypeStruct((4, 32, 1024), BF16),
            jax.ShapeDtypeStruct((768, 1024), BF16),
            jax.ShapeDtypeStruct((8, 1024), F32),
        ),
        in_specs=[in_vmem, in_vmem, pl.BlockSpec(memory_space=pl.ANY), in_vmem, in_vmem],
        out_specs=(in_vmem,) * 4,
        scratch_shapes=scratch,
        compiler_params=pltpu.CompilerParams(
            collective_id=0, has_side_effects=True, vmem_limit_bytes=60 * 1024 * 1024
        ),
        cost_estimate=pl.CostEstimate(flops=10_000_000_000, bytes_accessed=10_000_000, transcendentals=3_000_000),
    )(xs, cs, wb, sv, valid)


def per_device(
    inputs, lengths, cotangent, w_qkv, b_qv, w_out, w_up, b_up, w_down, norm_gains, norm_shifts, out_bias
):
    zh = lax.axis_index("section")
    zl = lax.axis_index("tensor") // 8
    xs = jnp.transpose(lax.dynamic_index_in_dim(inputs, zh, 0, keepdims=False), (1, 0, 2))
    cs = jnp.transpose(lax.dynamic_index_in_dim(cotangent, zh, 0, keepdims=False), (1, 0, 2))
    wb = jnp.concatenate(
        [jnp.transpose(w_qkv[0], (1, 2, 0)).reshape(192, 1024), w_out[0], w_up[0].T, w_down[0]], axis=0
    )
    zeros = jnp.zeros((64,), F32)
    up_row = lax.dynamic_update_slice(jnp.zeros((1024,), F32), b_up[0], (zl * 256,))
    qv_row = lax.dynamic_update_slice(
        jnp.zeros((1024,), F32), jnp.concatenate([b_qv[0, 0], zeros, b_qv[0, 1]]), (zl * 192,)
    )
    sv = jnp.concatenate([norm_gains[0], norm_shifts[0], out_bias[0], up_row[None], qv_row[None]], axis=0)
    length = lax.dynamic_slice(lengths, (zh, zl), (1, 1))
    r = lax.broadcasted_iota(jnp.int32, (512, 128), 0)
    position = ((r // 32) % 2) * 256 + (r // 64) * 32 + r % 32
    valid = (position < length).astype(F32)

    lout, igout, g, sm = run_kernel(xs, cs, wb, sv, valid)

    def place(blocks):
        return jnp.transpose(blocks.reshape(2, 2, 32, 1024), (0, 2, 1, 3))[None]

    g32 = g.astype(F32)
    grad_qkv = jnp.transpose(g32[0:192].reshape(3, 64, 1024), (2, 0, 1))[None]
    qv = lax.dynamic_slice(sm[7], (zl * 192,), (192,))
    up_bias = lax.dynamic_slice(sm[6], (zl * 256,), (256,))
    return (
        place(lout),
        place(igout).astype(F32),
        grad_qkv,
        jnp.stack([qv[0:64], qv[128:192]])[None],
        g32[192:256][None],
        g32[256:512].T[None],
        up_bias[None],
        g32[512:768][None],
        sm[0:2][None],
        sm[2:4][None],
        sm[4:6][None],
    )


def solution(mesh):
    in_specs = (
        P(None, "tensor", "dp", None),
        P(None, "dp"),
        P(None, "tensor", "dp", None),
        P("section", None, None, "tensor"),
        P("section", None, "tensor"),
        P("section", "tensor", None),
        P("section", None, "tensor"),
        P("section", "tensor"),
        P("section", "tensor", None),
        P("section", None, None),
        P("section", None, None),
        P("section", None, None),
    )
    out_specs = (
        P("section", None, "tensor", "dp", None),
        P("section", None, "tensor", "dp", None),
        P("section", None, None, "tensor"),
        P("section", None, "tensor"),
        P("section", "tensor", None),
        P("section", None, "tensor"),
        P("section", "tensor"),
        P("section", "tensor", None),
        P("section", None, None),
        P("section", None, None),
        P("section", None, None),
    )
    return jax.shard_map(per_device, mesh=mesh, in_specs=in_specs, out_specs=out_specs, check_vma=False)
```

time: 322 us -> 293 us (0.910)
  Pallas kernels: 292 us -> 266 us
    pallas_call x1, Pallas kernels: 292 us -> 266 us  [run_kernel(): pl.pallas_call(kernel, out_shape=(jax.ShapeDtypeStruct((4, 32, 1024), BF1...]
where the time goes in v2:
time: 293 us
  Pallas kernels  266 us (91%)
  local copies, waits for them, and re-layouts  20.1 us (7%)
  other arithmetic  6.15 us (2%)
    pallas_call x1, Pallas kernels, run_kernel(): pl.pallas_call(kernel, out_shape=(jax.ShapeDtypeStruct((4, 32, 1024), BF1...  266 us

profile of v2, /device:TPU:1, one launch (start us, length us, event | category | flops | bytes accessed | tf_op | source)
XLA Modules:
  0.0 292.6 jit_solution(4158574790005546910)
XLA Ops:
  0.7 1.3 dynamic_slice.18
  1.9 0.8 slice_bitcast_fusion.7
  2.7 0.1 pad_maximum_fusion.1
  2.8 0.7 constant_dynamic-update-slice_fusion
  3.5 0.1 dynamic_update_slice.9
  3.6 1.4 concatenate.11.sv
  5.0 2.6 fusion.5.valid
  7.6 1.1 constant_dynamic-slice_fusion.3
  8.8 0.7 copy.35
  9.5 0.7 copy.36
  10.1 1.2 copy.25
  11.4 2.5 pad_maximum_fusion.wb
  13.9 265.6 %shard_map.203 = (bf16[4,32,1024]{2,1,0:T(8,128)(2,1)}, bf16[4,32,1024]{2,1,0:T(8,128)(2,1)}, bf16[768,1024]{1,0:T(8,128)(2,1)}, f32[8,1024]{1,0:T(8,128)}) custom-call(bf16[2,32,1024]{2,1,0:T(8,128)(2,1)} %bitcast.73, bf16[2,32,1024]{2,1,0:T(8,128)(2,1)} %bitcast.72, bf16[768,1024]{1,0:T(8,128)(2,1)} %pad_maximum_fusion.wb, f32[8,1024]{1,0:T(8,128)} %concatenate.11.sv, ...), custom_call_target="tpu_custom_call" | custom-call | flops 10000000000 | bytes 10000000 | tf_op jit(solution)/shard_map/pallas_call | solution.py:638
  279.4 0.0 copy-start
  279.4 2.0 copy.34
  281.5 0.8 fusion.14
  282.3 1.5 slice_bitcast_fusion.3
  283.8 0.6 constant_dynamic-slice_fusion.1
  284.4 0.1 constant_dynamic-slice_fusion
  284.4 0.6 maximum_bitcast_fusion
  285.0 2.0 copy.33
  287.0 2.0 slice.54
  289.0 0.0 copy-done
  289.0 0.4 convert_element_type.23
  289.4 0.7 slice_bitcast_fusion.2
  290.1 1.2 slice_bitcast_fusion
  291.3 1.3 copy.28
  (8 shorter events, 0.0 us)
Async XLA Ops:
  279.4 9.6 %copy-start = (bf16[768,1024]{1,0:T(8,128)(2,1)S(1)}, bf16[768,1024]{1,0:T(8,128)(2,1)}, u32[]{:S(2)}) copy-start(bf16[768,1024]{1,0:T(8,128)(2,1)} %get-tuple-element.17) | copy-start | bytes 4718596

commit v3 on v2

--- a/solution.py
+++ b/solution.py
@@ -15,6 +15,8 @@
 SCALE = 0.125
 
 PIECES = ((0, 256), (256, 512))
+ALONG_Z = ((0, 128), (256, 192))
+QUARTERED = ((128, 128), (448, 320))
 
 
 def nt(a, b):
@@ -43,13 +45,14 @@
 
 
 def kernel(
-    xs, cs, wb, sv, valid,
-    lout, igout, gout, smout,
+    xs, cs, qkv_in, out_in, up_in, down_in, gains_in, shifts_in, bias_in, b_up_in, b_qv_in, len_in,
+    lout, igout, g_a, g_up, g_down, smout,
+    valid, sv, gout,
     W, SW, XF, YF, GF, GO, CT, PB, PT, PR, AT, HT, GD, GZT, GPT, GKT, GVT,
     N1, N2, S1, S2, Y1, GR, GY, OWN,
     PART, SIB, SUM, RIN, G, GXA, GXF, QXA, QXF, ZXA, ZXF,
     LO, IG, SM, SMC, SM1, SMY, SM2, SMZ, SM3, SMX,
-    ag_s, ag_r, sb_s, sb_r, rs_s, rs_r, in_s, in_r, loc, w_s, w_r,
+    ag_s, ag_r, sb_s, sb_r, rs_s, rs_r, in_s, in_r, loc, sv_s, sv_r, wz_s, wz_r, wq_s, wq_r, wx_s, wx_r,
     xr_s, xr_r, gz_s, gz_r, xg_s, xg_r, lo_s, lo_r, ig_s, ig_r,
     sc_s, sc_r, sy_s, sy_r, sz_s, sz_r, sx_s, sx_r,
 ):
@@ -193,45 +196,103 @@
 
     others = (far, cross, partner)
 
-    def w_at(l, b, i):
-        if i == 2:
-            return SW.at[2 * l + b]
-        base, size = PIECES[i]
-        return W.at[l, b, pl.ds(base, size)]
-
-    def w_copy(i, k):
-        src = sv if i == 2 else wb.at[pl.ds(*PIECES[i])]
-        return rc(src, w_at(zh, zl, i), w_s.at[k, i], w_r.at[zh, zl, i], others[k])
+    def sv_copy(k):
+        return rc(sv, SW.at[z], sv_s.at[k], sv_r.at[zh, zl], others[k])
+
+    def wz_copy(i, k):
+        rows = W.at[zh, zl, pl.ds(*ALONG_Z[i])]
+        return rc(rows, rows, wz_s.at[k, i], wz_r.at[zh, zl, i], others[k])
+
+    def quarter(l, b, i, who):
+        base, size = QUARTERED[i]
+        n = size // 4
+        return W.at[l, b, pl.ds(pl.multiple_of(base + who * n, 16), n)]
+
+    def wq_copy(i, k):
+        rows = quarter(zh, zl, i, x)
+        return rc(rows, rows, wq_s.at[k, i], wq_r.at[zh, zl, i], others[k])
+
+    def wx_copy(l, b, i, r):
+        rows = quarter(l, b, i, x)
+        return rc(rows, rows, wx_s.at[l, b, i, r - 1], wx_r.at[l, b, i, r - 1], xd(r))
 
     def send_own(i):
         for k in range(3):
-            w_copy(i, k).start()
+            wq_copy(i, k).start()
+        for k in range(3):
+            wz_copy(i, k).start()
+
+    def send_vectors():
+        for k in range(3):
+            sv_copy(k).start()
+
+    def pass_on(l, i):
+        for b in range(2):
+            @pl.when((2 * l + b) != z)
+            def _(b=b):
+                arrived(quarter(l, b, i, x), wq_r.at[l, b, i])
+                for r in (2, 1, 3):
+                    wx_copy(l, b, i, r).start()
+
+    def vectors_here(l):
+        for b in range(2):
+            @pl.when((2 * l + b) != z)
+            def _(b=b):
+                arrived(SW.at[2 * l + b], sv_r.at[l, b])
 
     def weights_here(l, i):
         for b in range(2):
             @pl.when((2 * l + b) != z)
             def _(b=b):
-                arrived(w_at(l, b, i), w_r.at[l, b, i])
+                arrived(W.at[l, b, pl.ds(*ALONG_Z[i])], wz_r.at[l, b, i])
+                for r in (1, 3, 2):
+                    arrived(quarter(l, b, i, lax.rem(x + 4 - r, 4)), wx_r.at[l, b, i, r - 1])
 
     mine_rows = pl.ds(pl.multiple_of(d * 64 + zl * 32, 32), 32)
     x_copy = rc(xs.at[1 - zl], XF.at[0, mine_rows], in_s.at[0], in_r.at[0], partner)
     x_copy.start()
     c_copy = rc(cs.at[1 - zl], CT.at[zl], in_s.at[1], in_r.at[1], partner)
 
+    own_block = W.at[zh, zl]
+    loads = [
+        pltpu.make_async_copy(src, own_block.at[pl.ds(base, size)], loc.at[i])
+        for i, (src, base, size) in enumerate(((qkv_in, 0, 192), (out_in, 192, 64), (down_in, 512, 256)))
+    ]
+    for load in loads:
+        load.start()
+    c_copy.start()
+    XF[0, mine_rows, :] = xs[zl]
+    CT[zl] = cs[zl]
+    first = zl == 0
+    sv[0:2, :] = gains_in[...]
+    sv[2:4, :] = shifts_in[...]
+    sv[4:6, :] = bias_in[...]
+    sv[6:8, :] = jnp.zeros((2, 1024), F32)
+    sv[6:7, 0:256] = jnp.where(first, b_up_in[...], 0.0)
+    sv[6:7, 256:512] = jnp.where(first, 0.0, b_up_in[...])
+    for i, at in ((0, 0), (1, 128)):
+        sv[7:8, at : at + 64] = jnp.where(first, b_qv_in[i : i + 1, :], 0.0)
+        sv[7:8, at + 192 : at + 256] = jnp.where(first, 0.0, b_qv_in[i : i + 1, :])
+    SW[z] = sv[...]
+    loads[0].wait()
+    loads[1].wait()
+
     @pl.when(zh == 0)
     def _():
-        send_own(2)
+        send_vectors()
         send_own(0)
+
+    own_block[256:512, :] = up_in[...].T
+    loads[2].wait()
+
+    @pl.when(zh == 0)
+    def _():
         send_own(1)
 
-    c_copy.start()
-    w_local = pltpu.make_async_copy(wb, W.at[zh, zl], loc)
-    w_local.start()
-    SW[z] = sv[...]
-    XF[0, mine_rows, :] = xs[zl]
-    CT[zl] = cs[zl]
+    r_ = lax.broadcasted_iota(jnp.int32, (512, 128), 0)
+    position = lax.rem(r_ // 32, 2) * 256 + (r_ // 64) * 32 + lax.rem(r_, 32)
+    valid[...] = jnp.where(position < len_in[zh, zl], 1.0, 0.0)
     arrived(XF.at[0, pl.ds(pl.multiple_of(d * 64 + (1 - zl) * 32, 32), 32)], in_r.at[0])
-    w_local.wait()
 
     def spread_out(rows, buf, out, s_s, s_r, l):
         buf[l] = rows.reshape(2, 32, 1024)
@@ -269,14 +330,24 @@
         return pl.ds(pl.multiple_of(yy * 128, 128), 128)
 
     def forward_layer(l, carry):
-        gather(XF, l, 0, lambda yy: None)
-        weights_here(l, 2)
+        seen = []
+
+        def between(yy):
+            seen.append(yy)
+            if len(seen) in (2, 4):
+                @pl.when(l == 0)
+                def _():
+                    pass_on(0, len(seen) // 2 - 1)
+
+        gather(XF, l, 0, between)
+        vectors_here(l)
         weights_here(l, 0)
 
         @pl.when((l == 0) & (zh == 1))
         def _():
-            send_own(2)
+            send_vectors()
             send_own(0)
+            send_own(1)
 
         qv_bias = SW[2 * l, 7:8, 0:384] + SW[2 * l + 1, 7:8, 0:384]
         proj = (nt(XF[l], qkv_weights(l)) + qv_bias).astype(BF16)
@@ -296,7 +367,13 @@
                 AT[l, h * 64 : h * 64 + 64, cols] = mixed.astype(BF16)
             return nn(AT[l, :, cols].T, out_weights(l))
 
-        attended = scatter(l, 0, attend, lambda: None)
+        def attend_window():
+            @pl.when(l == 0)
+            def _():
+                pass_on(1, 0)
+                pass_on(1, 1)
+
+        attended = scatter(l, 0, attend, attend_window)
         unit, inv = standardize(XF[l, own_rows, :].astype(F32) + attended + row_of(l, 4))
         N1[l] = unit
         S1[l] = jnp.broadcast_to(inv, (64, 128))
@@ -304,10 +381,6 @@
         Y1[...] = middle
         YF[l, own_rows, :] = middle.astype(BF16)
         weights_here(l, 1)
-
-        @pl.when((l == 0) & (zh == 1))
-        def _():
-            send_own(1)
 
         up_bias = SW[2 * l, 6:7, 0:512] + SW[2 * l + 1, 6:7, 0:512]
 
@@ -532,13 +605,25 @@
     spread_wait(LO, lout, lo_s, lo_r)
     spread_wait(IG, igout, ig_s, ig_r)
     grad_done(1)
+    g_up[...] = gout[256:512, :].T
+    g_down[...] = gout[512:768, :]
     grad_done(0)
+    g_a[...] = gout[0:256, :]
 
     x_copy.wait_send()
     c_copy.wait_send()
-    for i in range(3):
-        for k in range(3):
-            w_copy(i, k).wait_send()
+    for k in range(3):
+        sv_copy(k).wait_send()
+        for i in range(2):
+            wz_copy(i, k).wait_send()
+            wq_copy(i, k).wait_send()
+    for l in range(2):
+        for b in range(2):
+            @pl.when((2 * l + b) != z)
+            def _(l=l, b=b):
+                for i in range(2):
+                    for r in range(1, 4):
+                        wx_copy(l, b, i, r).wait_send()
     for p in range(2):
         for l in range(2):
             for b in range(2):
@@ -554,10 +639,13 @@
         cp.wait_send()
 
 
-def run_kernel(xs, cs, wb, sv, valid):
+def run_kernel(*operands):
     vm = pltpu.VMEM
     dma = pltpu.SemaphoreType.DMA
     scratch = [
+        vm((512, 128), F32),
+        vm((8, 1024), F32),
+        vm((768, 1024), BF16),
         vm((2, 2, 768, 1024), BF16),
         vm((4, 8, 1024), F32),
         vm((2, 512, 1024), BF16),
@@ -612,9 +700,15 @@
         dma((2, 4, 4)),
         dma((2,)),
         dma((2,)),
-        dma(()),
-        dma((3, 3)),
-        dma((2, 2, 3)),
+        dma((3,)),
+        dma((3,)),
+        dma((2, 2)),
+        dma((3, 2)),
+        dma((2, 2, 2)),
+        dma((3, 2)),
+        dma((2, 2, 2)),
+        dma((2, 2, 2, 3)),
+        dma((2, 2, 2, 3)),
         dma((2, 2, 2, 3)),
         dma((2, 2, 2, 3)),
         dma((2, 2, 2)),
@@ -635,22 +729,25 @@
         dma((4,)),
     ]
     in_vmem = pl.BlockSpec(memory_space=pltpu.VMEM)
+    hbm = pl.BlockSpec(memory_space=pl.ANY)
     return pl.pallas_call(
         kernel,
         out_shape=(
             jax.ShapeDtypeStruct((4, 32, 1024), BF16),
             jax.ShapeDtypeStruct((4, 32, 1024), BF16),
-            jax.ShapeDtypeStruct((768, 1024), BF16),
+            jax.ShapeDtypeStruct((256, 1024), BF16),
+            jax.ShapeDtypeStruct((1024, 256), BF16),
+            jax.ShapeDtypeStruct((256, 1024), BF16),
             jax.ShapeDtypeStruct((8, 1024), F32),
         ),
-        in_specs=[in_vmem, in_vmem, pl.BlockSpec(memory_space=pl.ANY), in_vmem, in_vmem],
-        out_specs=(in_vmem,) * 4,
+        in_specs=[in_vmem] * 2 + [hbm] * 2 + [in_vmem, hbm] + [in_vmem] * 5 + [pl.BlockSpec(memory_space=pltpu.SMEM)],
+        out_specs=(in_vmem,) * 6,
         scratch_shapes=scratch,
         compiler_params=pltpu.CompilerParams(
             collective_id=0, has_side_effects=True, vmem_limit_bytes=60 * 1024 * 1024
         ),
         cost_estimate=pl.CostEstimate(flops=10_000_000_000, bytes_accessed=10_000_000, transcendentals=3_000_000),
-    )(xs, cs, wb, sv, valid)
+    )(*operands)
 
 
 def per_device(
@@ -660,27 +757,15 @@
     zl = lax.axis_index("tensor") // 8
     xs = jnp.transpose(lax.dynamic_index_in_dim(inputs, zh, 0, keepdims=False), (1, 0, 2))
     cs = jnp.transpose(lax.dynamic_index_in_dim(cotangent, zh, 0, keepdims=False), (1, 0, 2))
-    wb = jnp.concatenate(
-        [jnp.transpose(w_qkv[0], (1, 2, 0)).reshape(192, 1024), w_out[0], w_up[0].T, w_down[0]], axis=0
+    qkv_rows = jnp.transpose(w_qkv[0], (1, 2, 0)).reshape(192, 1024)
+    lout, igout, g_a, g_up, g_down, sm = run_kernel(
+        xs, cs, qkv_rows, w_out[0], w_up[0], w_down[0], norm_gains[0], norm_shifts[0], out_bias[0], b_up, b_qv[0], lengths
     )
-    zeros = jnp.zeros((64,), F32)
-    up_row = lax.dynamic_update_slice(jnp.zeros((1024,), F32), b_up[0], (zl * 256,))
-    qv_row = lax.dynamic_update_slice(
-        jnp.zeros((1024,), F32), jnp.concatenate([b_qv[0, 0], zeros, b_qv[0, 1]]), (zl * 192,)
-    )
-    sv = jnp.concatenate([norm_gains[0], norm_shifts[0], out_bias[0], up_row[None], qv_row[None]], axis=0)
-    length = lax.dynamic_slice(lengths, (zh, zl), (1, 1))
-    r = lax.broadcasted_iota(jnp.int32, (512, 128), 0)
-    position = ((r // 32) % 2) * 256 + (r // 64) * 32 + r % 32
-    valid = (position < length).astype(F32)
-
-    lout, igout, g, sm = run_kernel(xs, cs, wb, sv, valid)
 
     def place(blocks):
         return jnp.transpose(blocks.reshape(2, 2, 32, 1024), (0, 2, 1, 3))[None]
 
-    g32 = g.astype(F32)
-    grad_qkv = jnp.transpose(g32[0:192].reshape(3, 64, 1024), (2, 0, 1))[None]
+    grad_qkv = jnp.transpose(g_a[0:192].astype(F32).reshape(3, 64, 1024), (2, 0, 1))[None]
     qv = lax.dynamic_slice(sm[7], (zl * 192,), (192,))
     up_bias = lax.dynamic_slice(sm[6], (zl * 256,), (256,))
     return (
@@ -688,10 +773,10 @@
         place(igout).astype(F32),
         grad_qkv,
         jnp.stack([qv[0:64], qv[128:192]])[None],
-        g32[192:256][None],
-        g32[256:512].T[None],
+        g_a[192:256].astype(F32)[None],
+        g_up.astype(F32)[None],
         up_bias[None],
-        g32[512:768][None],
+        g_down.astype(F32)[None],
         sm[0:2][None],
         sm[2:4][None],
         sm[4:6][None],

time: 293 us -> 256 us (0.87)
  Pallas kernels: 266 us -> 242 us
  local copies, waits for them, and re-layouts: 20.1 us -> 7.71 us
    pallas_call x1, Pallas kernels: 266 us -> 242 us  [run_kernel(): pl.pallas_call(kernel, out_shape=(jax.ShapeDtypeStruct((4, 32, 1024), BF1...]
    broadcast_in_dim x0 -> x4, other arithmetic: none -> 4.72 us  [the longest x1 1.62 us: per_device(): g_a[192:256].astype(F32)[None]]
    convert_element_type x2 -> x0, other arithmetic: 3 us -> none  [the longest x1 2.62 us: per_device(): valid = (position < length).astype(F32)]
where the time goes in v3:
time: 256 us
  Pallas kernels  242 us (95%)
  local copies, waits for them, and re-layouts  7.71 us (3%)
  other arithmetic  5.3 us (2%)
    pallas_call x1, Pallas kernels, run_kernel(): pl.pallas_call(kernel, out_shape=(jax.ShapeDtypeStruct((4, 32, 1024), BF1...  242 us

profile of v3, /device:TPU:1, one launch (start us, length us, event | category | flops | bytes accessed | tf_op | source)
XLA Modules:
  0.0 255.6 jit_solution(15945445748602452049)
XLA Ops:
  0.7 1.2 constant_dynamic-slice_fusion.3
  1.8 0.7 copy.33
  2.5 0.7 copy.34
  3.2 241.9 %shard_map.203 = (bf16[4,32,1024]{2,1,0:T(8,128)(2,1)}, bf16[4,32,1024]{2,1,0:T(8,128)(2,1)}, bf16[256,1024]{1,0:T(8,128)(2,1)}, bf16[1024,256]{1,0:T(8,128)(2,1...) custom-call(bf16[2,32,1024]{2,1,0:T(8,128)(2,1)} %bitcast.64, bf16[2,32,1024]{2,1,0:T(8,128)(2,1)} %bitcast.63, ...), custom_call_target="tpu_custom_call" | custom-call | flops 10000000000 | bytes 10000000 | tf_op jit(solution)/shard_map/pallas_call | solution.py:733
  245.1 0.0 copy-start.4
  245.1 0.9 fusion
  246.0 0.1 constant_dynamic-slice_fusion
  246.0 0.6 maximum_bitcast_fusion
  246.6 0.6 constant_dynamic-slice_fusion.1
  247.2 0.0 copy-done.4
  247.2 0.6 slice_bitcast_fusion
  247.8 1.0 slice.29
  248.8 0.0 copy-start.1
  248.8 1.0 convert_bitcast_fusion
  249.8 1.6 bitcast_convert_fusion.2
  251.4 0.0 copy-done.1
  251.4 0.0 copy-start
  251.4 1.1 bitcast_convert_fusion
  252.5 0.0 copy-done
  252.5 0.0 copy-start.2
  252.5 1.0 bitcast_convert_fusion.1
  253.6 0.0 copy-done.2
  253.6 0.0 copy-start.3
  253.6 1.1 copy.31
  254.6 0.0 copy-done.3
  254.6 1.0 copy.32
Async XLA Ops:
  245.1 2.1 copy-start.4
  248.8 2.6 %copy-start.1 = (bf16[256,1024]{1,0:T(8,128)(2,1)S(1)}, bf16[256,1024]{1,0:T(8,128)(2,1)}, u32[]{:S(2)}) copy-start(bf16[256,1024]{1,0:T(8,128)(2,1)} %get-tuple-element.22) | copy-start | bytes 1572868
  251.4 1.1 copy-start
  252.5 1.1 copy-start.2
  253.6 1.1 copy-start.3

commit v4 on v3

--- a/solution.py
+++ b/solution.py
@@ -46,12 +46,12 @@
 
 def kernel(
     xs, cs, qkv_in, out_in, up_in, down_in, gains_in, shifts_in, bias_in, b_up_in, b_qv_in, len_in,
-    lout, igout, g_a, g_up, g_down, smout,
-    valid, sv, gout,
-    W, SW, XF, YF, GF, GO, CT, PB, PT, PR, AT, HT, GD, GZT, GPT, GKT, GVT,
+    lout, igout, gout, smout,
+    valid, sv,
+    W, SW, XF, YF, GF, GO, CT, PB, PT, PR, AT, HT, GD, CDF, HB, GZT, GPT, GKT, GVT,
     N1, N2, S1, S2, Y1, GR, GY, OWN,
     PART, SIB, SUM, RIN, G, GXA, GXF, QXA, QXF, ZXA, ZXF,
-    LO, IG, SM, SMC, SM1, SMY, SM2, SMZ, SM3, SMX,
+    LO, IG, SM, SMN, SMC, SM1, SMY, SM2, SMZ, SM3, SMX,
     ag_s, ag_r, sb_s, sb_r, rs_s, rs_r, in_s, in_r, loc, sv_s, sv_r, wz_s, wz_r, wq_s, wq_r, wx_s, wx_r,
     xr_s, xr_r, gz_s, gz_r, xg_s, xg_r, lo_s, lo_r, ig_s, ig_r,
     sc_s, sc_r, sy_s, sy_r, sz_s, sz_r, sx_s, sx_r,
@@ -132,8 +132,7 @@
         use(lax.rem(y + 1, 4))
         from_sibling(full, l, k, 2)
         use(lax.rem(y + 2, 4))
-        for cp in copies:
-            cp.wait_send()
+        return copies
 
     def make(l, k, r, chunk, copies):
         PART[r] = chunk(lax.rem(y + r, 4)).astype(BF16)
@@ -147,52 +146,66 @@
         mine = PART[r, pl.ds(pl.multiple_of(c * 64, 64), 64), :]
         return mine.astype(F32) + SIB[r].astype(F32)
 
-    def push(l, k, r, copies):
+    def push(l, k, r, pushes):
         SUM[r] = both(l, k, r).astype(BF16)
         cp = rc(SUM.at[r], RIN.at[r], rs_s.at[l, k, r], rs_r.at[l, k, r], yd(r))
         cp.start()
-        copies.append(cp)
-
-    def finish(l, k, copies):
+        pushes.append(cp)
+
+    def finish(l, k, copies, pushes):
+        for cp in copies:
+            cp.wait_send()
         for r in (1, 3, 2):
             arrived(RIN.at[r], rs_r.at[l, k, r])
         total = OWN[...] + ((RIN[1].astype(F32) + RIN[3].astype(F32)) + RIN[2].astype(F32))
-        for cp in copies:
+        for cp in pushes:
             cp.wait_send()
         return total
 
-    def scatter(l, k, chunk, window):
-        copies = []
+    def scatter(l, k, chunk, window, copies, midway=lambda: None):
+        pushes = []
         make(l, k, 2, chunk, copies)
         make(l, k, 1, chunk, copies)
-        push(l, k, 2, copies)
+        push(l, k, 2, pushes)
         make(l, k, 3, chunk, copies)
-        push(l, k, 1, copies)
+        push(l, k, 1, pushes)
+        midway()
         make(l, k, 0, chunk, copies)
-        push(l, k, 3, copies)
+        push(l, k, 3, pushes)
         OWN[...] = both(l, k, 0)
         window()
-        return finish(l, k, copies)
+        return finish(l, k, copies, pushes)
 
     def gather_scatter(full, l, k, chunk, window):
-        copies = ag_begin(full, l, k)
+        mine = slot(full, l, y, c)
+        pushes = []
+
+        def to_ring(i):
+            return rc(mine, mine, ag_s.at[l, k, i], ag_r.at[l, k, i], yd(i))
+
+        copies = [rc(mine, mine, ag_s.at[l, k, 4], ag_r.at[l, k, 4], sibling), to_ring(1), to_ring(3)]
+        for cp in copies:
+            cp.start()
         from_sibling(full, l, k, 0)
         make(l, k, 0, chunk, copies)
+        cp = to_ring(2)
+        cp.start()
+        copies.append(cp)
         from_ring(full, l, k, 1, copies)
         from_ring(full, l, k, 3, copies)
         from_sibling(full, l, k, 1)
         make(l, k, 3, chunk, copies)
-        from_ring(full, l, k, 2, copies)
         from_sibling(full, l, k, 3)
         make(l, k, 1, chunk, copies)
-        push(l, k, 3, copies)
+        push(l, k, 3, pushes)
+        push(l, k, 1, pushes)
+        from_ring(full, l, k, 2, copies)
         from_sibling(full, l, k, 2)
         make(l, k, 2, chunk, copies)
-        push(l, k, 1, copies)
-        push(l, k, 2, copies)
+        push(l, k, 2, pushes)
         OWN[...] = both(l, k, 0)
         window()
-        return finish(l, k, copies)
+        return finish(l, k, copies, pushes)
 
     others = (far, cross, partner)
 
@@ -216,9 +229,11 @@
         rows = quarter(l, b, i, x)
         return rc(rows, rows, wx_s.at[l, b, i, r - 1], wx_r.at[l, b, i, r - 1], xd(r))
 
-    def send_own(i):
+    def send_quarter(i):
         for k in range(3):
             wq_copy(i, k).start()
+
+    def send_rest(i):
         for k in range(3):
             wz_copy(i, k).start()
 
@@ -280,15 +295,11 @@
     @pl.when(zh == 0)
     def _():
         send_vectors()
-        send_own(0)
+        send_quarter(0)
+        send_rest(0)
 
     own_block[256:512, :] = up_in[...].T
     loads[2].wait()
-
-    @pl.when(zh == 0)
-    def _():
-        send_own(1)
-
     r_ = lax.broadcasted_iota(jnp.int32, (512, 128), 0)
     position = lax.rem(r_ // 32, 2) * 256 + (r_ // 64) * 32 + lax.rem(r_, 32)
     valid[...] = jnp.where(position < len_in[zh, zl], 1.0, 0.0)
@@ -334,25 +345,28 @@
 
         def between(yy):
             seen.append(yy)
-            if len(seen) in (2, 4):
+            if len(seen) == 2:
+                @pl.when((l == 0) & (zh == 0))
+                def _():
+                    send_quarter(1)
+
                 @pl.when(l == 0)
                 def _():
-                    pass_on(0, len(seen) // 2 - 1)
-
-        gather(XF, l, 0, between)
+                    pass_on(0, 0)
+
+        x_copies = gather(XF, l, 0, between)
+
+        @pl.when((l == 0) & (zh == 0))
+        def _():
+            send_rest(1)
+
         vectors_here(l)
         weights_here(l, 0)
-
-        @pl.when((l == 0) & (zh == 1))
-        def _():
-            send_vectors()
-            send_own(0)
-            send_own(1)
-
         qv_bias = SW[2 * l, 7:8, 0:384] + SW[2 * l + 1, 7:8, 0:384]
         proj = (nt(XF[l], qkv_weights(l)) + qv_bias).astype(BF16)
         PB[l] = proj
         PT[l] = proj.T
+
 
         def attend(yy):
             cols = lanes(yy)
@@ -367,13 +381,20 @@
                 AT[l, h * 64 : h * 64 + 64, cols] = mixed.astype(BF16)
             return nn(AT[l, :, cols].T, out_weights(l))
 
-        def attend_window():
+        def attend_midway():
             @pl.when(l == 0)
             def _():
-                pass_on(1, 0)
-                pass_on(1, 1)
-
-        attended = scatter(l, 0, attend, attend_window)
+                pass_on(0, 1)
+
+        def attend_window():
+            @pl.when((l == 0) & (zh == 1))
+            def _():
+                send_vectors()
+                send_quarter(0)
+                send_rest(0)
+                send_quarter(1)
+
+        attended = scatter(l, 0, attend, attend_window, x_copies, attend_midway)
         unit, inv = standardize(XF[l, own_rows, :].astype(F32) + attended + row_of(l, 4))
         N1[l] = unit
         S1[l] = jnp.broadcast_to(inv, (64, 128))
@@ -391,13 +412,31 @@
                 pre = nt(rows, W[l, b, 256:512, :]) + up_bias[:, b * 256 : b * 256 + 256]
                 cdf = 0.5 * (1.0 + lax.erf(pre * INV_SQRT2))
                 hidden = (pre * cdf).astype(BF16)
-                GD[l, yy, :, b * 256 : b * 256 + 256] = cdf + pre * (INV_SQRT_2PI * jnp.exp(-0.5 * pre * pre))
-                HT[l, b * 256 : b * 256 + 256, lanes(yy)] = hidden.T
+                cols = pl.ds(b * 256, 256)
+                GD[l, yy, :, cols] = pre
+                CDF[yy, :, cols] = cdf
+                HB[yy, :, cols] = hidden
                 piece = nn(hidden, W[l, b, 512:768, :])
                 total = piece if total is None else total + piece
             return total
 
-        fed = gather_scatter(YF, l, 1, feed, lambda: None)
+        def feed_window():
+            @pl.loop(0, 4)
+            def _(yy):
+                HT[l, :, lanes(yy)] = HB[yy].T
+                pre = GD[l, yy]
+                GD[l, yy] = CDF[yy] + pre * (INV_SQRT_2PI * jnp.exp(-0.5 * pre * pre))
+
+            @pl.when(l == 0)
+            def _():
+                pass_on(1, 0)
+                pass_on(1, 1)
+
+            @pl.when((l == 0) & (zh == 1))
+            def _():
+                send_rest(1)
+
+        fed = gather_scatter(YF, l, 1, feed, feed_window)
         unit, inv = standardize(Y1[...] + fed + row_of(l, 5))
         N2[l] = unit
         S2[l] = jnp.broadcast_to(inv, (64, 128))
@@ -415,6 +454,9 @@
     arrived(CT.at[1 - zl], in_r.at[1])
     GY[...] = CT[...].reshape(64, 1024).astype(F32)
     SM[...] = jnp.zeros_like(SM)
+    SMN[...] = jnp.zeros_like(SMN)
+    norm_pair = rc(SMN, SMC, sc_s, sc_r, sibling)
+    norm_ring = [rc(SM1, SMY.at[y], sy_s.at[r], sy_r.at[r], yd(r)) for r in range(1, 4)]
 
     GX, QX, ZX = (GXA, GXF), (QXA, QXF), (ZXA, ZXF)
 
@@ -485,9 +527,9 @@
         grad = GY[...]
         unit = N2[l]
         grad_second = standardize_back(grad, row_of(l, 1), unit, S2[l, :, 0:1])
-        SM[l, 1:2, :] = jnp.sum(grad * unit, axis=0, keepdims=True)
-        SM[l, 3:4, :] = jnp.sum(grad, axis=0, keepdims=True)
-        SM[l, 5:6, :] = jnp.sum(grad_second, axis=0, keepdims=True)
+        SMN[l, 1:2, :] = jnp.sum(grad * unit, axis=0, keepdims=True)
+        SMN[l, 3:4, :] = jnp.sum(grad, axis=0, keepdims=True)
+        SMN[l, 5:6, :] = jnp.sum(grad_second, axis=0, keepdims=True)
         GR[...] = grad_second
         GF[l, own_rows, :] = grad_second.astype(BF16)
         def feed_back(yy):
@@ -495,13 +537,18 @@
             total = None
             for b in range(2):
                 grad_pre = (nt(rows, W[l, b, 512:768, :]) * GD[l, yy, :, b * 256 : b * 256 + 256]).astype(BF16)
-                SM[l, 6:7, b * 256 : b * 256 + 256] += jnp.sum(grad_pre.astype(F32), axis=0, keepdims=True)
-                GZT[b * 256 : b * 256 + 256, lanes(yy)] = grad_pre.T
+                HB[yy, :, pl.ds(b * 256, 256)] = grad_pre
                 piece = nn(grad_pre, W[l, b, 256:512, :])
                 total = piece if total is None else total + piece
             return total
 
         def feed_grads():
+            @pl.loop(0, 4)
+            def _(yy):
+                grad_pre = HB[yy]
+                GZT[:, lanes(yy)] = grad_pre.T
+                SM[l, 6:7, 0:512] += jnp.sum(grad_pre.astype(F32), axis=0, keepdims=True)
+
             @pl.loop(0, 2)
             def _(b):
                 rows = pl.ds(pl.multiple_of(b * 256, 256), 256)
@@ -518,9 +565,9 @@
         grad_middle = GR[...] + gather_scatter(GF, l, 2, feed_back, feed_grads)
         unit = N1[l]
         grad_first = standardize_back(grad_middle, row_of(l, 0), unit, S1[l, :, 0:1])
-        SM[l, 0:1, :] = jnp.sum(grad_middle * unit, axis=0, keepdims=True)
-        SM[l, 2:3, :] = jnp.sum(grad_middle, axis=0, keepdims=True)
-        SM[l, 4:5, :] = jnp.sum(grad_first, axis=0, keepdims=True)
+        SMN[l, 0:1, :] = jnp.sum(grad_middle * unit, axis=0, keepdims=True)
+        SMN[l, 2:3, :] = jnp.sum(grad_middle, axis=0, keepdims=True)
+        SMN[l, 4:5, :] = jnp.sum(grad_first, axis=0, keepdims=True)
         GR[...] = grad_first
         GO[l, own_rows, :] = grad_first.astype(BF16)
         GKT[...] = jnp.zeros_like(GKT)
@@ -543,17 +590,25 @@
                 GKT[h] += nt(PT[l, base : base + 64, cols], grad_score)
                 GVT[h] += nt(half, probs.astype(BF16))
 
-        gather(GO, l, 3, attend_back)
+        @pl.when(l == 0)
+        def _():
+            norm_pair.start()
+
+        o_copies = gather(GO, l, 3, attend_back)
+
+        @pl.when(l == 0)
+        def _():
+            arrived(SMC, sc_r)
+            SM1[...] = SMN[...] + SMC[...]
+            SMY[y] = SM1[...]
+            for cp in norm_ring:
+                cp.start()
+
 
         for h in range(2):
             base = h * 192
             GPT[base + 64 : base + 128, :] = (GKT[h] * SCALE).astype(BF16)
             GPT[base + 128 : base + 192, :] = GVT[h].astype(BF16)
-
-        def project_back(yy):
-            grad_proj = GPT[:, lanes(yy)].T
-            SM[l, 7:8, 0:384] += jnp.sum(grad_proj.astype(F32), axis=0, keepdims=True)
-            return nn(grad_proj, qkv_weights(l))
 
         def attend_grads():
             @pl.loop(0, 2)
@@ -563,7 +618,14 @@
 
             grad_x(l, 0)
 
-        grad_input = (GR[...] + scatter(l, 3, project_back, attend_grads)).astype(BF16)
+        pl.when(l == 0)(attend_grads)
+
+        def project_back(yy):
+            grad_proj = GPT[:, lanes(yy)].T
+            SM[l, 7:8, 0:384] += jnp.sum(grad_proj.astype(F32), axis=0, keepdims=True)
+            return nn(grad_proj, qkv_weights(l))
+
+        grad_input = (GR[...] + scatter(l, 3, project_back, lambda: pl.when(l == 1)(attend_grads), o_copies)).astype(BF16)
         GY[...] = grad_input.astype(F32)
         spread_out(grad_input, IG, igout, ig_s, ig_r, l)
         return carry
@@ -576,21 +638,14 @@
         cp.start()
         done.append(cp)
 
-    row = lax.broadcasted_iota(jnp.int32, (2, 8, 1024), 1)
-    go(rc(SM, SMC, sc_s, sc_r, sibling))
-    grad_z(0, 1)
-    arrived(SMC, sc_r)
-    SM1[...] = jnp.where(row < 6, SM[...] + SMC[...], SM[...])
-    SMY[y] = SM1[...]
-    for r in range(1, 4):
-        go(rc(SM1, SMY.at[y], sy_s.at[r], sy_r.at[r], yd(r)))
-    grad_z(0, 0)
     for r in range(1, 4):
         arrived(SMY.at[lax.rem(y + 4 - r, 4)], sy_r.at[r])
-    SM2[...] = jnp.where(row < 6, (SMY[0] + SMY[1]) + (SMY[2] + SMY[3]), SM1[...])
+    SM2[...] = ((SMY[0] + SMY[1]) + (SMY[2] + SMY[3])) + SM[...]
     SMZ[z] = SM2[zh]
     for k, where, lz in ((0, partner, zh), (1, cross, 1 - zh), (2, far, 1 - zh)):
         go(rc(SM2.at[lz], SMZ.at[z], sz_s.at[k], sz_r.at[k], where))
+    grad_z(0, 1)
+    grad_z(0, 0)
     grad_own(1)
     for k, zz in ((0, 2 * zh + 1 - zl), (1, 2 * (1 - zh) + 1 - zl), (2, 2 * (1 - zh) + zl)):
         arrived(SMZ.at[zz], sz_r.at[k])
@@ -601,14 +656,15 @@
     grad_own(0)
     for r in range(1, 4):
         arrived(SMX.at[lax.rem(x + 4 - r, 4)], sx_r.at[r])
-    smout[...] = (SMX[0] + SMX[1]) + (SMX[2] + SMX[3])
+    total = (SMX[0] + SMX[1]) + (SMX[2] + SMX[3])
+    first = zl == 0
+    smout[...] = total
+    smout[6:7, 0:256] = jnp.where(first, total[6:7, 0:256], total[6:7, 256:512])
+    smout[7:8, 0:192] = jnp.where(first, total[7:8, 0:192], total[7:8, 192:384])
     spread_wait(LO, lout, lo_s, lo_r)
     spread_wait(IG, igout, ig_s, ig_r)
     grad_done(1)
-    g_up[...] = gout[256:512, :].T
-    g_down[...] = gout[512:768, :]
     grad_done(0)
-    g_a[...] = gout[0:256, :]
 
     x_copy.wait_send()
     c_copy.wait_send()
@@ -635,7 +691,7 @@
                     z_copy_of(l, p, b).wait_send()
         for r in range(1, 4):
             g_copy_of(p, r).wait_send()
-    for cp in done:
+    for cp in done + [norm_pair] + norm_ring:
         cp.wait_send()
 
 
@@ -645,7 +701,6 @@
     scratch = [
         vm((512, 128), F32),
         vm((8, 1024), F32),
-        vm((768, 1024), BF16),
         vm((2, 2, 768, 1024), BF16),
         vm((4, 8, 1024), F32),
         vm((2, 512, 1024), BF16),
@@ -659,6 +714,8 @@
         vm((2, 128, 512), BF16),
         vm((2, 512, 512), BF16),
         vm((2, 4, 128, 512), F32),
+        vm((4, 128, 512), F32),
+        vm((4, 128, 512), BF16),
         vm((512, 512), BF16),
         vm((384, 512), BF16),
         vm((2, 64, 512), F32),
@@ -684,6 +741,7 @@
         vm((3, 128, 1024), BF16),
         vm((2, 2, 32, 1024), BF16),
         vm((2, 2, 32, 1024), BF16),
+        vm((2, 8, 1024), F32),
         vm((2, 8, 1024), F32),
         vm((2, 8, 1024), F32),
         vm((2, 8, 1024), F32),
@@ -735,19 +793,71 @@
         out_shape=(
             jax.ShapeDtypeStruct((4, 32, 1024), BF16),
             jax.ShapeDtypeStruct((4, 32, 1024), BF16),
-            jax.ShapeDtypeStruct((256, 1024), BF16),
-            jax.ShapeDtypeStruct((1024, 256), BF16),
-            jax.ShapeDtypeStruct((256, 1024), BF16),
+            jax.ShapeDtypeStruct((768, 1024), BF16),
             jax.ShapeDtypeStruct((8, 1024), F32),
         ),
         in_specs=[in_vmem] * 2 + [hbm] * 2 + [in_vmem, hbm] + [in_vmem] * 5 + [pl.BlockSpec(memory_space=pltpu.SMEM)],
-        out_specs=(in_vmem,) * 6,
+        out_specs=(in_vmem,) * 4,
         scratch_shapes=scratch,
         compiler_params=pltpu.CompilerParams(
             collective_id=0, has_side_effects=True, vmem_limit_bytes=60 * 1024 * 1024
         ),
         cost_estimate=pl.CostEstimate(flops=10_000_000_000, bytes_accessed=10_000_000, transcendentals=3_000_000),
     )(*operands)
+
+
+def place_kernel(
+    lout_in, igout_in, gout_in, sm_in,
+    out, grad_in, qkv, qv, w_out, up, up_bias, down, gains, shifts, bias,
+    lout, igout, gout, sm, sems,
+):
+    pairs = ((gout_in, gout), (igout_in, igout), (lout_in, lout), (sm_in, sm))
+    loads = [pltpu.make_async_copy(src, dst, sems.at[i]) for i, (src, dst) in enumerate(pairs)]
+    for load in loads:
+        load.start()
+    for load in loads:
+        load.wait()
+    for m in range(2):
+        for q in range(2):
+            grad_in[0, m, :, q, :] = igout[2 * m + q].astype(F32)
+    out[0] = jnp.transpose(lout[...].reshape(2, 2, 32, 1024), (0, 2, 1, 3))
+    qkv[...] = gout[0:192, :].astype(F32)
+    w_out[0] = gout[192:256, :].astype(F32)
+    up[0] = gout[256:512, :].astype(F32).T
+    down[0] = gout[512:768, :].astype(F32)
+    gains[0] = sm[0:2, :]
+    shifts[0] = sm[2:4, :]
+    bias[0] = sm[4:6, :]
+    up_bias[...] = sm[6:7, 0:256]
+    qv[0, 0:1, :] = sm[7:8, 0:64]
+    qv[0, 1:2, :] = sm[7:8, 128:192]
+
+
+def place_outputs(lout, igout, gout, sm):
+    vmem = pl.BlockSpec(memory_space=pltpu.VMEM)
+
+    def f32(*shape):
+        return jax.ShapeDtypeStruct(shape, F32)
+
+    return pl.pallas_call(
+        place_kernel,
+        out_shape=(
+            jax.ShapeDtypeStruct((1, 2, 32, 2, 1024), BF16), f32(1, 2, 32, 2, 1024), f32(192, 1024), f32(1, 2, 64),
+            f32(1, 64, 1024), f32(1, 1024, 256), f32(1, 256), f32(1, 256, 1024),
+            f32(1, 2, 1024), f32(1, 2, 1024), f32(1, 2, 1024),
+        ),
+        in_specs=[pl.BlockSpec(memory_space=pl.ANY)] * 4,
+        out_specs=(vmem,) * 11,
+        scratch_shapes=[
+            pltpu.VMEM((4, 32, 1024), BF16),
+            pltpu.VMEM((4, 32, 1024), BF16),
+            pltpu.VMEM((768, 1024), BF16),
+            pltpu.VMEM((8, 1024), F32),
+            pltpu.SemaphoreType.DMA((4,)),
+        ],
+        compiler_params=pltpu.CompilerParams(vmem_limit_bytes=60 * 1024 * 1024),
+        cost_estimate=pl.CostEstimate(flops=1_000_000, bytes_accessed=6_000_000, transcendentals=0),
+    )(lout, igout, gout, sm)
 
 
 def per_device(
@@ -758,29 +868,14 @@
     xs = jnp.transpose(lax.dynamic_index_in_dim(inputs, zh, 0, keepdims=False), (1, 0, 2))
     cs = jnp.transpose(lax.dynamic_index_in_dim(cotangent, zh, 0, keepdims=False), (1, 0, 2))
     qkv_rows = jnp.transpose(w_qkv[0], (1, 2, 0)).reshape(192, 1024)
-    lout, igout, g_a, g_up, g_down, sm = run_kernel(
-        xs, cs, qkv_rows, w_out[0], w_up[0], w_down[0], norm_gains[0], norm_shifts[0], out_bias[0], b_up, b_qv[0], lengths
+    out, grad_in, qkv, qv, g_out, up, up_bias, down, gains, shifts, bias = place_outputs(
+        *run_kernel(
+            xs, cs, qkv_rows, w_out[0], w_up[0], w_down[0],
+            norm_gains[0], norm_shifts[0], out_bias[0], b_up, b_qv[0], lengths,
+        )
     )
-
-    def place(blocks):
-        return jnp.transpose(blocks.reshape(2, 2, 32, 1024), (0, 2, 1, 3))[None]
-
-    grad_qkv = jnp.transpose(g_a[0:192].astype(F32).reshape(3, 64, 1024), (2, 0, 1))[None]
-    qv = lax.dynamic_slice(sm[7], (zl * 192,), (192,))
-    up_bias = lax.dynamic_slice(sm[6], (zl * 256,), (256,))
-    return (
-        place(lout),
-        place(igout).astype(F32),
-        grad_qkv,
-        jnp.stack([qv[0:64], qv[128:192]])[None],
-        g_a[192:256].astype(F32)[None],
-        g_up.astype(F32)[None],
-        up_bias[None],
-        g_down.astype(F32)[None],
-        sm[0:2][None],
-        sm[2:4][None],
-        sm[4:6][None],
-    )
+    grad_qkv = jnp.transpose(qkv.reshape(3, 64, 1024), (2, 0, 1))[None]
+    return (out, grad_in, grad_qkv, qv, g_out, up, up_bias, down, gains, shifts, bias)
 
 
 def solution(mesh):

time: 256 us -> 238 us (0.930)
  Pallas kernels: 242 us -> 235 us
  other arithmetic: 5.3 us -> 0 us
  local copies, waits for them, and re-layouts: 7.71 us -> 2.51 us
    pallas_call x1, Pallas kernels: 242 us -> 231 us  [run_kernel(): pl.pallas_call(kernel, out_shape=(jax.ShapeDtypeStruct((4, 32, 1024), BF1...]
    broadcast_in_dim x5 -> x0, other arithmetic: 5.3 us -> none  [the longest x1 1.62 us: per_device(): g_a[192:256].astype(F32)[None]]
    pallas_call x0 -> x1, Pallas kernels: none -> 3.68 us  [place_outputs(): pl.pallas_call(place_kernel, out_shape=(jax.ShapeDtypeStruct((1, 2, 32, 2...]
where the time goes in v4:
time: 238 us
  Pallas kernels  235 us (99%)
  local copies, waits for them, and re-layouts  2.51 us (1%)
    pallas_call x1, Pallas kernels, run_kernel(): pl.pallas_call(kernel, out_shape=(jax.ShapeDtypeStruct((4, 32, 1024), BF1...  231 us

profile of v4, /device:TPU:1, one launch (start us, length us, event | category | flops | bytes accessed | tf_op | source)
XLA Modules:
  0.0 238.0 jit_solution(14568501678676859068)
XLA Ops:
  0.6 1.2 constant_dynamic-slice_fusion
  1.8 0.7 copy.27
  2.5 0.7 copy.28
  3.2 230.9 %shard_map.203 = (bf16[4,32,1024]{2,1,0:T(8,128)(2,1)}, bf16[4,32,1024]{2,1,0:T(8,128)(2,1)}, bf16[768,1024]{1,0:T(8,128)(2,1)}, f32[8,1024]{1,0:T(8,128)}) custom-call(bf16[2,32,1024]{2,1,0:T(8,128)(2,1)} %bitcast.28, bf16[2,32,1024]{2,1,0:T(8,128)(2,1)} %bitcast.27, bf16[192,1024]{1,0:T(8,128)(2,1)} %bitcast.32, bf16[64,1024]{1,0:T(8,128)(2,1)} %bitcast.33, ...), custom_call_target="tpu_custom_call" | custom-call | flops 10000000000 | bytes 10000000 | tf_op jit(solution)/shard_map/pallas_call | solution.py:791
  234.1 3.7 %shard_map.204 = (bf16[1,2,32,2,1024]{4,3,2,1,0:T(2,128)(2,1)}, f32[1,2,32,2,1024]{4,3,2,1,0:T(2,128)}, f32[192,1024]{1,0:T(8,128)}, f32[1,2,64]{2,1,0:T(2,128)}...) custom-call(bf16[4,32,1024]{2,1,0:T(8,128)(2,1)} %get-tuple-element., ...), custom_call_target="tpu_custom_call" | custom-call | flops 1000000 | bytes 6000000 | tf_op jit(solution)/shard_map/pallas_call | solution.py:842

commit v5 on v4

--- a/solution.py
+++ b/solution.py
@@ -53,7 +53,7 @@
     PART, SIB, SUM, RIN, G, GXA, GXF, QXA, QXF, ZXA, ZXF,
     LO, IG, SM, SMN, SMC, SM1, SMY, SM2, SMZ, SM3, SMX,
     ag_s, ag_r, sb_s, sb_r, rs_s, rs_r, in_s, in_r, loc, sv_s, sv_r, wz_s, wz_r, wq_s, wq_r, wx_s, wx_r,
-    xr_s, xr_r, gz_s, gz_r, xg_s, xg_r, lo_s, lo_r, ig_s, ig_r,
+    xr_s, xr_r, xf_s, xf_r, xa_s, xa_r, gz_s, gz_r, xg_s, xg_r, lo_s, lo_r, ig_s, ig_r,
     sc_s, sc_r, sy_s, sy_r, sz_s, sz_r, sx_s, sx_r,
 ):
     zh = lax.axis_index("section")
@@ -458,44 +458,84 @@
     norm_pair = rc(SMN, SMC, sc_s, sc_r, sibling)
     norm_ring = [rc(SM1, SMY.at[y], sy_s.at[r], sy_r.at[r], yd(r)) for r in range(1, 4)]
 
-    GX, QX, ZX = (GXA, GXF), (QXA, QXF), (ZXA, ZXF)
+    QX, ZX = (QXA, QXF), (ZXA, ZXF)
 
     def own_part(p, ref, who, *lead):
         base, size = PIECES[p]
         n = size // 4
         return ref.at[(*lead, pl.ds(pl.multiple_of(base + who * n, n), n))]
 
-    def x_copy_of(l, p, b, r):
-        src = own_part(p, G, lax.rem(x + r, 4), l, b)
-        return rc(src, GX[p].at[l, b, r - 1], xr_s.at[l, p, b, r - 1], xr_r.at[l, p, b, r - 1], xd(r))
+    def x_copy_of(l, b, r):
+        src = own_part(0, G, lax.rem(x + r, 4), l, b)
+        return rc(src, GXA.at[l, b, r - 1], xr_s.at[l, b, r - 1], xr_r.at[l, b, r - 1], xd(r))
+
+    def half_of(ref, r, half, *lead):
+        start = 256 + lax.rem(x + r, 4) * 128 + half * 64
+        return ref.at[(*lead, pl.ds(pl.multiple_of(start, 64), 64))]
+
+    RING = ((2, 0, 1), (2, 1, 3), (1, 1, 1), (3, 0, 3), (1, 0, 1), (3, 1, 3))
+
+    def ring_copy(l, b, i):
+        r, half, to = RING[i]
+        return rc(half_of(G, r, half, l, b), GXF.at[l, b, i], xf_s.at[l, b, i], xf_r.at[l, b, i], xd(to))
+
+    def ring_first(l):
+        for i in range(4):
+            for b in range(2):
+                ring_copy(l, b, i).start()
+
+    def ring_second(l):
+        for i in range(2):
+            for b in range(2):
+                arrived(GXF.at[l, b, i], xf_r.at[l, b, i])
+                r, half, _ = RING[4 + i]
+                mine = half_of(G, r, half, l, b)
+                mine[...] = (mine[...].astype(F32) + GXF[l, b, i].astype(F32)).astype(BF16)
+                ring_copy(l, b, 4 + i).start()
 
     def z_copy_of(l, p, b):
         k = lax.rem(2 * l + b + 4 - z, 4) - 1
         return rc(QX[p].at[l, b], ZX[p].at[k], gz_s.at[l, p, b], gz_r.at[p, k], dev(zh_=l, zl_=b))
 
-    def g_copy_of(p, r):
-        mine = own_part(p, gout, x)
-        return rc(mine, mine, xg_s.at[p, r - 1], xg_r.at[p, r - 1], xd(r))
-
-    def grad_x(l, p):
+    def g_copy_of(r):
+        mine = own_part(0, gout, x)
+        return rc(mine, mine, xg_s.at[r - 1], xg_r.at[r - 1], xd(r))
+
+    AROUND = ((0, 0, 1), (0, 1, 3), (0, 1, 1), (0, 0, 3), (3, 0, 1), (1, 1, 3))
+
+    def around(i):
+        r, half, to = AROUND[i]
+        rows = half_of(gout, r, half)
+        return rc(rows, rows, xa_s.at[i], xa_r.at[i], xd(to))
+
+    def around_here(i):
+        r, half, to = AROUND[i]
+        arrived(half_of(gout, r + 4 - to, half), xa_r.at[i])
+
+    def grad_x(l):
         for b in range(2):
             for r in (2, 1, 3):
-                x_copy_of(l, p, b, r).start()
+                x_copy_of(l, b, r).start()
 
     def grad_z(l, p):
-        n = PIECES[p][1] // 4
         for b in range(2):
-            for r in (1, 3, 2):
-                arrived(GX[p].at[l, b, r - 1], xr_r.at[l, p, b, r - 1])
             mine = own_part(p, G, x, l, b)
-
-            @pl.loop(0, n // 32)
-            def _(i, b=b, mine=mine):
-                rows = pl.ds(pl.multiple_of(i * 32, 32), 32)
-                QX[p][l, b, rows, :] = (
-                    (mine[rows, :].astype(F32) + GX[p][l, b, 0, rows, :].astype(F32))
-                    + (GX[p][l, b, 1, rows, :].astype(F32) + GX[p][l, b, 2, rows, :].astype(F32))
-                ).astype(BF16)
+            if p == 0:
+                for r in (1, 3, 2):
+                    arrived(GXA.at[l, b, r - 1], xr_r.at[l, b, r - 1])
+                got = ((0, 64, tuple(GXA.at[l, b, i] for i in range(3))),)
+            else:
+                for i in (2, 3, 4, 5):
+                    arrived(GXF.at[l, b, i], xf_r.at[l, b, i])
+                got = (
+                    (0, 64, (GXF.at[l, b, 3], GXF.at[l, b, 4])),
+                    (64, 64, (GXF.at[l, b, 2], GXF.at[l, b, 5])),
+                )
+            for base, size, terms in got:
+                total = mine[base : base + size, :].astype(F32)
+                for term in terms:
+                    total = total + term[...].astype(F32)
+                QX[p][l, b, base : base + size, :] = total.astype(BF16)
 
             @pl.when((2 * l + b) != z)
             def _(b=b):
@@ -515,12 +555,21 @@
                 + (ZX[p][1, rows, :].astype(F32) + ZX[p][2, rows, :].astype(F32))
             ).astype(BF16)
 
-        for r in (2, 1, 3):
-            g_copy_of(p, r).start()
-
-    def grad_done(p):
+        if p == 0:
+            for r in (2, 1, 3):
+                g_copy_of(r).start()
+        else:
+            for i in range(4):
+                around(i).start()
+
+    def grad_done():
+        for i in (0, 1):
+            around_here(i)
+            around(4 + i).start()
+        for i in (2, 3, 4, 5):
+            around_here(i)
         for r in (1, 3, 2):
-            arrived(own_part(p, gout, lax.rem(x + 4 - r, 4)), xg_r.at[p, r - 1])
+            arrived(own_part(0, gout, lax.rem(x + 4 - r, 4)), xg_r.at[r - 1])
 
     def backward_layer(step, carry):
         l = 1 - step
@@ -555,7 +604,7 @@
                 G[l, b, 256:512, :] = nn(GZT[rows, :], YF[l]).astype(BF16)
                 G[l, b, 512:768, :] = nn(HT[l, rows, :], GF[l]).astype(BF16)
 
-            grad_x(l, 1)
+            ring_first(l)
 
             @pl.when(l == 0)
             def _():
@@ -595,6 +644,7 @@
             norm_pair.start()
 
         o_copies = gather(GO, l, 3, attend_back)
+        ring_second(l)
 
         @pl.when(l == 0)
         def _():
@@ -616,7 +666,7 @@
                 G[l, b, 0:192, :] = nn(GPT[pl.ds(pl.multiple_of(b * 192, 64), 192), :], XF[l]).astype(BF16)
                 G[l, b, 192:256, :] = nn(AT[l, pl.ds(pl.multiple_of(b * 64, 64), 64), :], GO[l]).astype(BF16)
 
-            grad_x(l, 0)
+            grad_x(l)
 
         pl.when(l == 0)(attend_grads)
 
@@ -625,7 +675,14 @@
             SM[l, 7:8, 0:384] += jnp.sum(grad_proj.astype(F32), axis=0, keepdims=True)
             return nn(grad_proj, qkv_weights(l))
 
-        grad_input = (GR[...] + scatter(l, 3, project_back, lambda: pl.when(l == 1)(attend_grads), o_copies)).astype(BF16)
+        def project_window():
+            pl.when(l == 1)(attend_grads)
+
+            @pl.when(l == 0)
+            def _():
+                grad_z(0, 1)
+
+        grad_input = (GR[...] + scatter(l, 3, project_back, project_window, o_copies)).astype(BF16)
         GY[...] = grad_input.astype(F32)
         spread_out(grad_input, IG, igout, ig_s, ig_r, l)
         return carry
@@ -638,14 +695,13 @@
         cp.start()
         done.append(cp)
 
+    grad_z(0, 0)
     for r in range(1, 4):
         arrived(SMY.at[lax.rem(y + 4 - r, 4)], sy_r.at[r])
     SM2[...] = ((SMY[0] + SMY[1]) + (SMY[2] + SMY[3])) + SM[...]
     SMZ[z] = SM2[zh]
     for k, where, lz in ((0, partner, zh), (1, cross, 1 - zh), (2, far, 1 - zh)):
         go(rc(SM2.at[lz], SMZ.at[z], sz_s.at[k], sz_r.at[k], where))
-    grad_z(0, 1)
-    grad_z(0, 0)
     grad_own(1)
     for k, zz in ((0, 2 * zh + 1 - zl), (1, 2 * (1 - zh) + 1 - zl), (2, 2 * (1 - zh) + zl)):
         arrived(SMZ.at[zz], sz_r.at[k])
@@ -663,8 +719,7 @@
     smout[7:8, 0:192] = jnp.where(first, total[7:8, 0:192], total[7:8, 192:384])
     spread_wait(LO, lout, lo_s, lo_r)
     spread_wait(IG, igout, ig_s, ig_r)
-    grad_done(1)
-    grad_done(0)
+    grad_done()
 
     x_copy.wait_send()
     c_copy.wait_send()
@@ -680,17 +735,21 @@
                 for i in range(2):
                     for r in range(1, 4):
                         wx_copy(l, b, i, r).wait_send()
-    for p in range(2):
-        for l in range(2):
-            for b in range(2):
-                for r in range(1, 4):
-                    x_copy_of(l, p, b, r).wait_send()
-
-                @pl.when((2 * l + b) != z)
-                def _(l=l, b=b, p=p):
+    for l in range(2):
+        for b in range(2):
+            for r in range(1, 4):
+                x_copy_of(l, b, r).wait_send()
+            for i in range(6):
+                ring_copy(l, b, i).wait_send()
+
+            @pl.when((2 * l + b) != z)
+            def _(l=l, b=b):
+                for p in range(2):
                     z_copy_of(l, p, b).wait_send()
-        for r in range(1, 4):
-            g_copy_of(p, r).wait_send()
+    for r in range(1, 4):
+        g_copy_of(r).wait_send()
+    for i in range(6):
+        around(i).wait_send()
     for cp in done + [norm_pair] + norm_ring:
         cp.wait_send()
 
@@ -734,7 +793,7 @@
         vm((4, 64, 1024), BF16),
         vm((2, 2, 768, 1024), BF16),
         vm((2, 2, 3, 64, 1024), BF16),
-        vm((2, 2, 3, 128, 1024), BF16),
+        vm((2, 2, 6, 64, 1024), BF16),
         vm((2, 2, 64, 1024), BF16),
         vm((2, 2, 128, 1024), BF16),
         vm((3, 64, 1024), BF16),
@@ -767,12 +826,16 @@
         dma((2, 2, 2)),
         dma((2, 2, 2, 3)),
         dma((2, 2, 2, 3)),
-        dma((2, 2, 2, 3)),
-        dma((2, 2, 2, 3)),
+        dma((2, 2, 3)),
+        dma((2, 2, 3)),
+        dma((2, 2, 6)),
+        dma((2, 2, 6)),
+        dma((6,)),
+        dma((6,)),
         dma((2, 2, 2)),
         dma((2, 3)),
-        dma((2, 3)),
-        dma((2, 3)),
+        dma((3,)),
+        dma((3,)),
         dma((2, 2)),
         dma((4,)),
         dma((2, 2)),

time: 238 us -> 230 us (0.966)
  Pallas kernels: 235 us -> 225 us
    pallas_call x1, Pallas kernels: 231 us -> 222 us  [run_kernel(): pl.pallas_call(kernel, out_shape=(jax.ShapeDtypeStruct((4, 32, 1024), BF1...]
where the time goes in v5:
time: 230 us; the launch traced here: 229 us
  Pallas kernels  225 us (98%)
  local copies, waits for them, and re-layouts  2.51 us (1%)
    pallas_call x1, Pallas kernels, run_kernel(): pl.pallas_call(kernel, out_shape=(jax.ShapeDtypeStruct((4, 32, 1024), BF1...  222 us

profile of v5, /device:TPU:1, one launch (start us, length us, event | category | flops | bytes accessed | tf_op | source)
XLA Modules:
  0.0 228.6 jit_solution(14592602207665394041)
XLA Ops:
  0.6 1.2 constant_dynamic-slice_fusion
  1.8 0.7 copy.27
  2.5 0.7 copy.28
  3.2 221.6 %shard_map.203 = (bf16[4,32,1024]{2,1,0:T(8,128)(2,1)}, bf16[4,32,1024]{2,1,0:T(8,128)(2,1)}, bf16[768,1024]{1,0:T(8,128)(2,1)}, f32[8,1024]{1,0:T(8,128)}) custom-call(bf16[2,32,1024]{2,1,0:T(8,128)(2,1)} %bitcast.28, bf16[2,32,1024]{2,1,0:T(8,128)(2,1)} %bitcast.27, bf16[192,1024]{1,0:T(8,128)(2,1)} %bitcast.32, bf16[64,1024]{1,0:T(8,128)(2,1)} %bitcast.33, ...), custom_call_target="tpu_custom_call" | custom-call | flops 10000000000 | bytes 10000000 | tf_op jit(solution)/shard_map/pallas_call | solution.py:854
  224.8 3.7 %shard_map.204 = (bf16[1,2,32,2,1024]{4,3,2,1,0:T(2,128)(2,1)}, f32[1,2,32,2,1024]{4,3,2,1,0:T(2,128)}, f32[192,1024]{1,0:T(8,128)}, f32[1,2,64]{2,1,0:T(2,128)}...) custom-call(bf16[4,32,1024]{2,1,0:T(8,128)(2,1)} %get-tuple-element., ...), custom_call_target="tpu_custom_call" | custom-call | flops 1000000 | bytes 6000000 | tf_op jit(solution)/shard_map/pallas_call | solution.py:905

commit v6 on v5

--- a/solution.py
+++ b/solution.py
@@ -345,7 +345,7 @@
 
         def between(yy):
             seen.append(yy)
-            if len(seen) == 2:
+            if len(seen) == 3:
                 @pl.when((l == 0) & (zh == 0))
                 def _():
                     send_quarter(1)

time: 230 us -> 229 us (level)
  no operation moved by 1% of the time
where the time goes in v6:
time: 229 us
  Pallas kernels  225 us (98%)
  local copies, waits for them, and re-layouts  2.51 us (1%)
    pallas_call x1, Pallas kernels, run_kernel(): pl.pallas_call(kernel, out_shape=(jax.ShapeDtypeStruct((4, 32, 1024), BF1...  222 us

profile of v6, /device:TPU:1, one launch (start us, length us, event | category | flops | bytes accessed | tf_op | source)
XLA Modules:
  0.0 228.6 jit_solution(17711446096829291193)
XLA Ops:
  0.6 1.2 constant_dynamic-slice_fusion
  1.8 0.7 copy.27
  2.5 0.7 copy.28
  3.2 221.6 %shard_map.203 = (bf16[4,32,1024]{2,1,0:T(8,128)(2,1)}, bf16[4,32,1024]{2,1,0:T(8,128)(2,1)}, bf16[768,1024]{1,0:T(8,128)(2,1)}, f32[8,1024]{1,0:T(8,128)}) custom-call(bf16[2,32,1024]{2,1,0:T(8,128)(2,1)} %bitcast.28, bf16[2,32,1024]{2,1,0:T(8,128)(2,1)} %bitcast.27, bf16[192,1024]{1,0:T(8,128)(2,1)} %bitcast.32, bf16[64,1024]{1,0:T(8,128)(2,1)} %bitcast.33, ...), custom_call_target="tpu_custom_call" | custom-call | flops 10000000000 | bytes 10000000 | tf_op jit(solution)/shard_map/pallas_call | solution.py:854
  224.8 3.7 %shard_map.204 = (bf16[1,2,32,2,1024]{4,3,2,1,0:T(2,128)(2,1)}, f32[1,2,32,2,1024]{4,3,2,1,0:T(2,128)}, f32[192,1024]{1,0:T(8,128)}, f32[1,2,64]{2,1,0:T(2,128)}...) custom-call(bf16[4,32,1024]{2,1,0:T(8,128)(2,1)} %get-tuple-element., ...), custom_call_target="tpu_custom_call" | custom-call | flops 1000000 | bytes 6000000 | tf_op jit(solution)/shard_map/pallas_call | solution.py:905
